TPU v7x, 128 devices: a whole 4x4x4 slice. The times are simulated.
128 devices in a mesh: wide: 16 (over x, y), sub: 8 (over z, core).
Axes of the slice: x: 4, y: 4, z: 4, core: 2. Of those that a mesh axis runs over, the one named last changes fastest.
Arguments:
- krylov_basis: float32 [4, 16384, 16, 128], P(None, ('wide', 'sub')), may hold values from -5 to 5
- quad_weight: float32 [16384, 128], P(('wide', 'sub')), may hold values from 0.5 to 18
- corrections: bfloat16 [16384, 3, 128, 128], P(('wide', 'sub')), may hold values from -0.3125 to 0.3125
- patch_route: int32 [16384, 1], P(('wide', 'sub')), may hold values from 0 to 7; in each aligned block of 128 rows (0 to 127, 128 to 255, ...) at most 64 rows name the same one
- leaf_slot: int32 [16384], P(('wide', 'sub')), may hold values from 0 to 7
- multipole_map: bfloat16 [128, 256], replicated, may hold values from -0.5 to 0.5
- upward_translation: float32 [1024, 256, 256], P(('wide', 'sub')), may hold values from -0.375 to 0.375
- far_coupling: float32 [16, 16, 256, 256], P('wide', None, 'sub'), may hold values from -0.09375 to 0.09375
- downward_translation: float32 [1024, 256, 256], P(('wide', 'sub')), may hold values from -0.375 to 0.375
- evaluation_map: bfloat16 [256, 128], replicated, may hold values from -0.375 to 0.375
Outputs:
- new_vector: float32 [16384, 16, 128], P(('wide', 'sub'))
- hessenberg: float32 [5, 16], replicated
Inputs may be any that keep to these rules, and one draw needn't show every extreme that they name: `patch_route`: within each aligned block of the 128 patches of one device, at most 64 patches share a value.
All inputs are finite; a program needn't handle non-finite values.
Results may differ from a plain program's by a relative error of at most 0.004.
Values may be sent and summed in bfloat16 or wider, within the bound.
A program may use at most 128 MiB of HBM per device.

v0:
```python
import math

import jax
import jax.numpy as jnp
from jax import lax
from jax.sharding import PartitionSpec as P

HIGHEST = lax.Precision.HIGHEST


def shifted(value, axis, steps):
    count = lax.axis_size(axis)
    initial, last = (max(0, -steps), min(count, count - steps))
    return lax.ppermute(value, axis, [(source, source + steps) for source in range(initial, last)])


def weighted_products(basis_set, vector, weights, total_nodes):
    return (
        jnp.einsum("jprq,prq,pq->jr", basis_set, vector, weights, precision=HIGHEST) / total_nodes
    )


def weighted_square(vector, weights, total_nodes):
    return jnp.einsum("prq,prq,pq->r", vector, vector, weights, precision=HIGHEST) / total_nodes


def per_device(
    krylov_basis,
    quad_weight,
    corrections,
    patch_route,
    leaf_slot,
    multipole_map,
    upward_translation,
    far_coupling,
    downward_translation,
    evaluation_map,
):
    sub_count = lax.axis_size("sub")
    wide_count = lax.axis_size("wide")
    patch_count = corrections.shape[0]
    node_count = corrections.shape[2]
    rhs_count = krylov_basis.shape[2]
    leaf_count = upward_translation.shape[0]
    capacity = 4 * patch_count // sub_count
    slot_count = sub_count * capacity
    total_nodes = float(patch_count * node_count * sub_count * wide_count)
    current = krylov_basis[-1]
    current_half = current.astype(jnp.bfloat16)
    partials = jnp.einsum(
        "pra,pjab->pjrb", current_half, corrections, preferred_element_type=jnp.float32
    )
    to_lower = shifted(partials[0, 0], ("wide", "sub"), -1)
    to_upper = shifted(partials[-1, 2], ("wide", "sub"), 1)
    from_above = jnp.concatenate([partials[1:, 0], to_lower[None]], axis=0)
    from_below = jnp.concatenate([to_upper[None], partials[:-1, 2]], axis=0)
    near_field = partials[:, 1] + from_above + from_below
    density_scale = 1.0 / math.sqrt(patch_count * sub_count)
    weighted = (current * quad_weight[:, None, :] * density_scale).astype(jnp.bfloat16)
    dest_sub = patch_route[:, 0]
    dest_hot = (dest_sub[:, None] == jnp.arange(sub_count, dtype=jnp.int32)[None, :]).astype(
        jnp.int32
    )
    before = jnp.sum((jnp.cumsum(dest_hot, axis=0) - dest_hot) * dest_hot, axis=1)
    position = dest_sub * capacity + before
    slot_ids = jnp.arange(slot_count, dtype=jnp.int32)
    dispatch = (slot_ids[:, None] == position[None, :]).astype(jnp.bfloat16)
    collect = (position[:, None] == slot_ids[None, :]).astype(jnp.bfloat16)
    packed = jnp.dot(
        dispatch,
        weighted.reshape(patch_count, rhs_count * node_count),
        preferred_element_type=jnp.float32,
    ).astype(jnp.bfloat16)
    labels = jnp.dot(
        dispatch, (leaf_slot + 1).astype(jnp.bfloat16)[:, None], preferred_element_type=jnp.float32
    ).astype(jnp.bfloat16)
    arrived, arrived_labels = (
        lax.all_to_all(
            packed.reshape(sub_count, capacity, rhs_count * node_count),
            "sub",
            split_axis=0,
            concat_axis=0,
            tiled=True,
        ),
        lax.all_to_all(
            labels.reshape(sub_count, capacity, 1), "sub", split_axis=0, concat_axis=0, tiled=True
        ),
    )
    slot_rows = arrived.reshape(slot_count, rhs_count, node_count)
    expanded = jnp.einsum(
        "nrq,qk->nrk", slot_rows, multipole_map, preferred_element_type=jnp.float32
    )
    slot_leaf = arrived_labels.reshape(slot_count).astype(jnp.int32) - 1
    leaf_ids = jnp.arange(leaf_count, dtype=jnp.int32)
    leaf_hot = (leaf_ids[:, None] == slot_leaf[None, :]).astype(jnp.float32)
    moments = jnp.einsum("ln,nrk->lrk", leaf_hot, expanded, precision=HIGHEST)
    tree_part = jnp.einsum("lrk,lkc->rc", moments, upward_translation, precision=HIGHEST)
    tree_share = lax.psum_scatter(tree_part, "sub", scatter_dimension=1, tiled=True)
    all_trees = lax.all_gather(tree_share[None], "wide", axis=0, tiled=True)
    local_part = jnp.einsum("wrk,wkc->rc", all_trees, far_coupling[0], precision=HIGHEST)
    local_exp = lax.psum(local_part, "sub")
    leaf_terms = jnp.einsum(
        "rk,lkc->lrc", local_exp, downward_translation, precision=HIGHEST
    ).astype(jnp.bfloat16)
    leaf_field = jnp.einsum(
        "lrk,kq->lrq", leaf_terms, evaluation_map, preferred_element_type=jnp.float32
    ).astype(jnp.bfloat16)
    slot_hot = (slot_leaf[:, None] == leaf_ids[None, :]).astype(jnp.bfloat16)
    slot_field = jnp.dot(
        slot_hot,
        leaf_field.reshape(leaf_count, rhs_count * node_count),
        preferred_element_type=jnp.float32,
    ).astype(jnp.bfloat16)
    returned = lax.all_to_all(
        slot_field.reshape(sub_count, capacity, rhs_count * node_count),
        "sub",
        split_axis=0,
        concat_axis=0,
        tiled=True,
    )
    far_half = (
        jnp.dot(
            collect,
            returned.reshape(slot_count, rhs_count * node_count),
            preferred_element_type=jnp.float32,
        )
        .astype(jnp.bfloat16)
        .reshape(patch_count, rhs_count, node_count)
    )
    far_field = lax.optimization_barrier(far_half).astype(jnp.float32)
    operator_out = 0.5 * current + near_field + far_field
    first_pass = lax.psum(
        weighted_products(krylov_basis, operator_out, quad_weight, total_nodes), ("wide", "sub")
    )
    after_first = operator_out - jnp.einsum(
        "jr,jprq->prq", first_pass, krylov_basis, precision=HIGHEST
    )
    second_pass = lax.psum(
        weighted_products(krylov_basis, after_first, quad_weight, total_nodes), ("wide", "sub")
    )
    remainder = after_first - jnp.einsum(
        "jr,jprq->prq", second_pass, krylov_basis, precision=HIGHEST
    )
    square_sum = lax.psum(weighted_square(remainder, quad_weight, total_nodes), ("wide", "sub"))
    coefficients = first_pass + second_pass
    beta_norm = jnp.sqrt(square_sum + 1e-06)
    new_vector = remainder / beta_norm[None, :, None]
    hessenberg = jnp.concatenate([coefficients, beta_norm[None]], axis=0)
    return (new_vector, hessenberg)


def solution(mesh):
    return jax.shard_map(
        per_device,
        mesh=mesh,
        in_specs=(
            P(None, ("wide", "sub"), None, None),
            P(("wide", "sub"), None),
            P(("wide", "sub"), None, None, None),
            P(("wide", "sub"), None),
            P(("wide", "sub")),
            P(),
            P(("wide", "sub"), None, None),
            P("wide", None, "sub", None),
            P(("wide", "sub"), None, None),
            P(),
        ),
        out_specs=(P(("wide", "sub"), None, None), P()),
        check_vma=False,
    )
```

profile of v0, /device:TPU:1, one launch (start us, length us, event | category | flops | bytes accessed | tf_op | source)
XLA Modules:
  0.0 469.0 jit_solution(6179353871716518090)
XLA Ops:
  11.3 6.8 %all-to-all-start = ((bf16[8,64,1]{1,2,0:T(2,128)(2,1)}), bf16[8,64,1]{1,2,0:T(2,128)(2,1)S(1)}, u32[]{:S(2)}, u32[]{:S(2)}) async-start(bf16[8,64,1]{1,2,0:T(2,128)(2,1)} %reshape.91), calls=%async_computation | async-start | bytes 8192 | tf_op jit(solution)/shard_map/all_to_all | solution.py:85
  19.0 2.4 convolution_convert_fusion.1
  22.6 5.0 %all-to-all-start.1 = ((bf16[8,64,2048]{2,1,0:T(8,128)(2,1)}), bf16[8,64,2048]{2,1,0:T(8,128)(2,1)}, u32[]{:S(2)}, u32[]{:S(2)}) async-start(bf16[8,64,2048]{2,1,0:T(8,128)(2,1)} %bitcast.158), calls=%async_computation.1 | async-start | bytes 4194304 | tf_op jit(solution)/shard_map/all_to_all | solution.py:78
  27.7 26.4 %all-to-all-done.1 = bf16[8,64,2048]{2,1,0:T(8,128)(2,1)} async-done(((bf16[8,64,2048]{2,1,0:T(8,128)(2,1)}), bf16[8,64,2048]{2,1,0:T(8,128)(2,1)}, u32[]{:S(2)}, u32[]{:S(2)}) %all-to-all-start.1) | async-done | bytes 2097184 | tf_op jit(solution)/shard_map/all_to_all | solution.py:78
  54.1 2.2 copy.41
  57.6 2.8 fusion.45
  60.4 4.1 convolution_bitcast_fusion
  64.5 27.5 %reduce-scatter.4.cloned.1.call-done = f32[32,16]{1,0:T(8,128)} async-done(((f32[256,16]{1,0:T(8,128)}), f32[32,16]{1,0:T(8,128)}) %reduce-scatter.4.cloned.1.call-update) | async-done | bytes 2064
  92.8 18.7 %all-gather = f32[256,32]{1,0:T(8,128)S(1)} all-gather(f32[16,32]{1,0:T(8,128)S(1)} %copy.38), channel_id=2, replica_groups=mesh['wide'=16,'sub'=8] {'wide'}, dimensions={0}, use_global_device_ids=true | all-gather | bytes 34816 | tf_op jit(solution)/shard_map/all_gather | solution.py:99
  112.0 28.7 %psum.28 = f32[16,256]{1,0:T(8,128)S(1)} all-reduce(f32[16,256]{1,0:T(8,128)S(1)} %convolution_bitcast_fusion.1), channel_id=1, replica_groups=mesh['wide'=16,'sub'=8] {'sub'}, use_global_device_ids=true, to_apply=%region_3.4 | all-reduce | flops 4096 | bytes 32768 | tf_op jit(solution)/shard_map/psum | solution.py:101
  144.1 7.8 %all-to-all-start.2 = ((bf16[8,64,2048]{2,1,0:T(8,128)(2,1)}), bf16[8,64,2048]{2,1,0:T(8,128)(2,1)}, u32[]{:S(2)}, u32[]{:S(2)}) async-start(bf16[8,64,2048]{2,1,0:T(8,128)(2,1)} %bitcast.157), calls=%async_computation.2 | async-start | bytes 4194304 | tf_op jit(solution)/shard_map/all_to_all | solution.py:114
  151.9 7.2 %fusion.12 = f32[128,3,16,128]{3,2,0,1:T(8,128)S(1)} fusion(bf16[128,3,128,128]{3,2,1,0:T(8,128)(2,1)} %param.12, f32[4,128,16,128]{3,2,1,0:T(8,128)} %param.10), kind=kOutput, calls=%fused_computation.15 | convolution fusion | flops 201326592 | bytes 16252928 | tf_op jit(solution)/shard_map/pra,pjab->pjrb/dot_general | solution.py:50
  159.1 3.7 collective-permute-start.1
  165.9 12.5 %all-to-all-done.2 = bf16[8,64,2048]{2,1,0:T(8,128)(2,1)} async-done(((bf16[8,64,2048]{2,1,0:T(8,128)(2,1)}), bf16[8,64,2048]{2,1,0:T(8,128)(2,1)}, u32[]{:S(2)}, u32[]{:S(2)}) %all-to-all-start.2) | async-done | bytes 2097184 | tf_op jit(solution)/shard_map/all_to_all | solution.py:114
  178.3 2.2 fusion.15
  180.7 3.0 multiply_bitcast_fusion.1
  183.7 31.9 %fusion.8 = f32[16,1,4,1]{2,1,3,0:T(1,128)S(1)} fusion(f32[4,128,16,128]{3,2,1,0:T(8,128)S(1)} %copy-done.1, f32[128,128,16,1]{1,2,0,3:T(8,128)S(1)} %get-tuple-element.2), kind=kOutput, calls=%fused_computation.10 | convolution fusion | flops 12582912 | bytes 5243136 | tf_op jit(solution)/shard_map/jprq,prq,pq->jr/dot_general | solution.py:19
  215.7 64.1 %psum.29 = f32[4,16]{1,0:T(4,128)S(1)} all-reduce(f32[4,16]{1,0:T(4,128)S(1)} %fusion.49), channel_id=1, replica_groups=mesh['wide'=16,'sub'=8] {'wide','sub'}, use_global_device_ids=true, to_apply=%region_4.5 | all-reduce | flops 64 | bytes 512 | tf_op jit(solution)/shard_map/psum | solution.py:132
  279.9 13.1 %fusion.6 = f32[16,1,128,128]{3,1,2,0:T(1,128)S(1)} fusion(f32[4,16,1,1]{0,2,3,1:T(1,128)S(1)} %copy.25, f32[4,128,16,128]{3,2,1,0:T(8,128)} %param.10), kind=kOutput, calls=%fused_computation.8 | convolution fusion | flops 12582912 | bytes 5243136 | tf_op jit(solution)/shard_map/jr,jprq->prq/dot_general | solution.py:135
  293.7 23.2 %fusion.4 = f32[16,1,4,1]{2,1,3,0:T(1,128)S(1)} fusion(f32[4,128,16,128]{3,2,1,0:T(8,128)S(1)} %copy-done.2, f32[128,128,16,1]{1,2,0,3:T(8,128)S(1)} %multiply_bitcast_fusion), kind=kOutput, calls=%fused_computation.6 | convolution fusion | flops 12582912 | bytes 5243136 | tf_op jit(solution)/shard_map/jprq,prq,pq->jr/dot_general | solution.py:19
  317.0 62.6 %psum.30 = f32[4,16]{1,0:T(4,128)S(1)} all-reduce(f32[4,16]{1,0:T(4,128)S(1)} %fusion.48), channel_id=1, replica_groups=mesh['wide'=16,'sub'=8] {'wide','sub'}, use_global_device_ids=true, to_apply=%region_5.6 | all-reduce | flops 64 | bytes 512 | tf_op jit(solution)/shard_map/psum | solution.py:138
  379.6 12.6 %fusion.2 = f32[16,1,128,128]{3,1,2,0:T(1,128)S(1)} fusion(f32[4,16,1,1]{0,2,3,1:T(1,128)S(1)} %copy.29, f32[4,128,16,128]{3,2,1,0:T(8,128)} %param.10), kind=kOutput, calls=%fused_computation.4 | convolution fusion | flops 12582912 | bytes 5243136 | tf_op jit(solution)/shard_map/jr,jprq->prq/dot_general | solution.py:141
  393.7 64.1 %psum.31 = f32[16]{0:T(128)S(1)} all-reduce(f32[16]{0:T(128)S(1)} %broadcast_multiply_fusion), channel_id=1, replica_groups=mesh['wide'=16,'sub'=8] {'wide','sub'}, use_global_device_ids=true, to_apply=%region_6.7 | all-reduce | flops 16 | bytes 128 | tf_op jit(solution)/shard_map/psum | solution.py:144
  457.7 3.7 broadcast_divide_fusion
  (68 shorter events, 18.4 us)
Async XLA Ops:
  7.2 133.6 %copy-start = (f32[8,256,256]{2,1,0:T(8,128)S(1)}, f32[8,256,256]{2,1,0:T(8,128)}, u32[]{:S(2)}) copy-start(f32[8,256,256]{2,1,0:T(8,128)} %param.18) | copy-start | bytes 6291460
  7.2 11.8 %slice-start = ((f32[4,128,16,128]{3,2,1,0:T(8,128)}), f32[1,128,16,128]{3,2,1,0:T(8,128)S(1)}, s32[]{:S(2)}) async-start(f32[4,128,16,128]{3,2,1,0:T(8,128)} %param.10), calls=%async_computation.5 | async-start | bytes 2097152 | tf_op jit(solution)/shard_map/slice | solution.py:48
  11.3 11.3 %all-to-all-start = ((bf16[8,64,1]{1,2,0:T(2,128)(2,1)}), bf16[8,64,1]{1,2,0:T(2,128)(2,1)S(1)}, u32[]{:S(2)}, u32[]{:S(2)}) async-start(bf16[8,64,1]{1,2,0:T(2,128)(2,1)} %reshape.91), calls=%async_computation | async-start | bytes 8192 | tf_op jit(solution)/shard_map/all_to_all | solution.py:85
  22.6 33.7 %copy-start.11 = (bf16[128,256]{1,0:T(8,128)(2,1)S(1)}, bf16[128,256]{1,0:T(8,128)(2,1)}, u32[]{:S(2)}) copy-start(bf16[128,256]{1,0:T(8,128)(2,1)} %param.15) | copy-start | bytes 196612
  22.6 31.5 %all-to-all-start.1 = ((bf16[8,64,2048]{2,1,0:T(8,128)(2,1)}), bf16[8,64,2048]{2,1,0:T(8,128)(2,1)}, u32[]{:S(2)}, u32[]{:S(2)}) async-start(bf16[8,64,2048]{2,1,0:T(8,128)(2,1)} %bitcast.158), calls=%async_computation.1 | async-start | bytes 4194304 | tf_op jit(solution)/shard_map/all_to_all | solution.py:78
  27.6 64.4 %reduce-scatter.4.cloned.1.call-start = ((), (), s32[]{:S(2)}) async-start(), calls=%async_computation.4 | async-start | bytes 147456
  57.5 2.9 copy-start.8
  57.6 54.0 %copy-start.10 = (f32[1,16,32,256]{3,2,1,0:T(8,128)S(1)}, f32[1,16,32,256]{3,2,1,0:T(8,128)}, u32[]{:S(2)}) copy-start(f32[1,16,32,256]{3,2,1,0:T(8,128)} %param.17) | copy-start | bytes 1572868
  60.4 81.4 %copy-start.12 = (bf16[256,128]{1,0:T(8,128)(2,1)S(1)}, bf16[256,128]{1,0:T(8,128)(2,1)}, u32[]{:S(2)}) copy-start(bf16[256,128]{1,0:T(8,128)(2,1)} %param.19) | copy-start | bytes 196612
  144.1 34.2 %all-to-all-start.2 = ((bf16[8,64,2048]{2,1,0:T(8,128)(2,1)}), bf16[8,64,2048]{2,1,0:T(8,128)(2,1)}, u32[]{:S(2)}, u32[]{:S(2)}) async-start(bf16[8,64,2048]{2,1,0:T(8,128)(2,1)} %bitcast.157), calls=%async_computation.2 | async-start | bytes 4194304 | tf_op jit(solution)/shard_map/all_to_all | solution.py:114
  151.9 12.9 %copy-start.13 = (s32[128,1]{0,1:T(1,128)S(1)}, s32[128,1]{0,1:T(1,128)}, u32[]{:S(2)}) copy-start(s32[128,1]{0,1:T(1,128)} %param.13) | copy-start | bytes 1540
  159.1 5.7 %copy-start.6 = (f32[128,3,16,128]{3,2,0,1:T(8,128)}, f32[128,3,16,128]{3,2,0,1:T(8,128)S(1)}, u32[]{:S(2)}) copy-start(f32[128,3,16,128]{3,2,0,1:T(8,128)S(1)} %fusion.12) | copy-start | bytes 9437188
  159.1 21.6 %copy-start.9 = (f32[128,128]{1,0:T(8,128)S(1)}, f32[128,128]{1,0:T(8,128)}, u32[]{:S(2)}) copy-start(f32[128,128]{1,0:T(8,128)} %param.11) | copy-start | bytes 196612
  159.1 21.5 %collective-permute-start.1 = (f32[16,128]{1,0:T(8,128)S(1)}, f32[16,128]{1,0:T(8,128)S(1)}, u32[]{:S(2)}, u32[]{:S(2)}) collective-permute-start(f32[16,128]{1,0:T(8,128)S(1)} %get-tuple-element.7), channel_id=1, source_target_pairs={{0,1},{1,2},{2,3},{3,4},{4,5},{5,6},{6,7},{7,8},{8,9},{9,10},{10,1... | collective-permute-start | bytes 24584 | tf_op jit(solution)/shard_map/ppermute | solution.py:14
  162.8 17.9 %collective-permute-start = (f32[16,128]{1,0:T(8,128)S(1)}, f32[16,128]{1,0:T(8,128)S(1)}, u32[]{:S(2)}, u32[]{:S(2)}) collective-permute-start(f32[16,128]{1,0:T(8,128)S(1)} %get-tuple-element.6), channel_id=1, source_target_pairs={{1,0},{2,1},{3,2},{4,3},{5,4},{6,5},{7,6},{8,7},{9,8},{10,9},{11,1... | collective-permute-start | bytes 24584 | tf_op jit(solution)/shard_map/ppermute | solution.py:14
  178.3 2.3 copy-start.7
  180.5 3.2 copy-start.1
  279.9 13.1 %copy-start.3 = (f32[128,16,128]{2,1,0:T(8,128)S(1)}, f32[128,16,128]{2,1,0:T(8,128)}, u32[]{:S(2)}) copy-start(f32[128,16,128]{2,1,0:T(8,128)} %get-tuple-element.3) | copy-start | bytes 3145732
  279.9 13.8 %copy-start.2 = (f32[4,128,16,128]{3,2,1,0:T(8,128)S(1)}, f32[4,128,16,128]{3,2,1,0:T(8,128)}, u32[]{:S(2)}) copy-start(f32[4,128,16,128]{3,2,1,0:T(8,128)} %param.10) | copy-start | bytes 12582916
  379.6 12.7 %copy-start.4 = (f32[128,16,128]{2,1,0:T(8,128)S(1)}, f32[128,16,128]{2,1,0:T(8,128)}, u32[]{:S(2)}) copy-start(f32[128,16,128]{2,1,0:T(8,128)} %get-tuple-element.3) | copy-start | bytes 3145732
  392.3 1.4 copy-start.5
Sparse Core Ops, SparseCore 0:
  64.6 27.3 reduce-scatter.3
where the time goes:
time: 479 us; the launch traced here: 469 us
  blocking collectives  238 us (50%)
  matrix products  105 us (22%)
  waiting for transfers between devices  67.6 us (14%)
  starting transfers between devices  25.2 us (5%)
  between operations  14.5 us (3%)
  other arithmetic  12 us (3%)
  local copies, waits for them, and re-layouts  6.27 us (1%)
    psum x1, blocking collectives, per_device(): lax.psum(weighted_products(krylov_basis, operator_out, quad_weight, total...  64.1 us
    psum x1, blocking collectives, per_device(): lax.psum(weighted_square(remainder, quad_weight, total_nodes), ('wide', '...  64.1 us
    psum x1, blocking collectives, per_device(): lax.psum(weighted_products(krylov_basis, after_first, quad_weight, total_...  62.6 us
    dot_general x2, matrix products, weighted_products(): jnp.einsum('jprq,prq,pq->jr', basis_set, vector, weights, precision=HIGHEST)  55 us
    psum x1, blocking collectives, per_device(): local_exp = lax.psum(local_part, 'sub')  28.7 us
    unnamed x2, waiting for transfers between devices  27.5 us
    all_to_all x1, waiting for transfers between devices, per_device(): lax.all_to_all(packed.reshape(sub_count, capacity, rhs_count * node_count...  26.4 us
    all_gather x1, blocking collectives, per_device(): all_trees = lax.all_gather(tree_share[None], 'wide', axis=0, tiled=True)  18.7 us
  transfers between devices with their start and end apart: 6, of which 4 were waited for; matrix products, arithmetic and copies ran while one was open for 3% of the time, Pallas kernels for 0%

commit v1 on v0

v1 whole, which is shorter than its diff:
```python
import functools

import jax
import jax.numpy as jnp
from jax import lax
from jax.experimental import pallas as pl
from jax.experimental.pallas import tpu as pltpu
from jax.sharding import PartitionSpec as P

MESH = pl.DeviceIdType.MESH
F32 = jnp.float32
BF16 = jnp.bfloat16
WIDE, SUB = 16, 8
PATCHES, RHS, NODES, COEFFS, BASIS, LEAVES = 128, 16, 128, 256, 4, 8
SHARE = COEFFS // SUB
ROWS = PATCHES * RHS
TOTAL = float(WIDE * SUB * PATCHES * NODES)
SCALE = 1.0 / 32.0
PAIRS = [(j, k) for j in range(BASIS) for k in range(j, BASIS)]
NEAR_CHUNKS = 4


def split(value):
    high = value.astype(BF16)
    return high, (value - high.astype(F32)).astype(BF16)


def dot(a, b):
    return jnp.dot(a, b, preferred_element_type=F32)


def split_dot(value, high_ref, low_ref):
    high, low = split(value)
    rows = value.shape[0]
    both = dot(jnp.concatenate([high, low], axis=0), high_ref[...])
    return both[:rows] + both[rows:] + dot(high, low_ref[...])


def patch_rows(p):
    return pl.ds(pl.multiple_of(p * RHS, RHS), RHS)


def kernel(
    basis_hbm, weight_hbm, corr_hbm, route_hbm, slot_hbm, multi_hbm, up_hbm, far_hbm, down_hbm,
    eval_hbm, vector_out, hess_out,
    basis, weight, corr, route_v, slot_v, route_s, slot_s, multi, up, far, down, evalm, edge_corr,
    up_high, up_low, far_high, far_low, down_high, down_low, image,
    send1, recv1, sums1, send2, recv2, send3, recv3, send4, recv4, field,
    edge_send, edge_recv, send6, recv6, send7, recv7,
    load_sem, corr_sem, edge_s, edge_r, s1, r1, s2, r2, s3, r3, s4, r4, s5, r5, s6, r6, s7, r7,
):
    w = lax.axis_index("wide")
    s = lax.axis_index("sub")
    me = w * SUB + s
    below = lax.rem(me + WIDE * SUB - 1, WIDE * SUB)
    above = lax.rem(me + 1, WIDE * SUB)
    below_id = (below // SUB, lax.rem(below, SUB))
    above_id = (above // SUB, lax.rem(above, SUB))
    subs = [lax.rem(s + d, SUB) for d in range(1, SUB)]
    wides = [lax.rem(w + d, WIDE) for d in range(1, WIDE)]
    wide_sources = [lax.rem(w + WIDE - d, WIDE) for d in range(1, WIDE)]

    barrier = pltpu.get_barrier_semaphore()
    peers = [(w, t) for t in subs] + [(v, s) for v in wides] + [below_id, above_id]
    for peer in peers:
        pl.semaphore_signal(barrier, inc=1, device_id=peer, device_id_type=MESH)

    last = BASIS - 1
    loads = {}

    def load(name, source, target):
        copy = pltpu.make_async_copy(source, target, load_sem.at[len(loads)])
        copy.start()
        loads[name] = copy

    load("current", basis_hbm.at[last], basis.at[last])
    load("weight", weight_hbm, weight)
    load("route_v", route_hbm, route_v)
    load("slot_v", slot_hbm, slot_v)
    load("multi", multi_hbm, multi)
    load("up", up_hbm, up)
    load("edge0", corr_hbm.at[0], edge_corr.at[0])
    load("edge1", corr_hbm.at[3 * PATCHES - 1], edge_corr.at[1])
    load("route_s", route_hbm, route_s)
    load("slot_s", slot_hbm, slot_s)
    load("far", far_hbm, far)
    load("eval", eval_hbm, evalm)
    load("down", down_hbm, down)
    blocks = 3 * PATCHES // NEAR_CHUNKS
    corr_loads = []
    for c in range(NEAR_CHUNKS):
        copy = pltpu.make_async_copy(
            corr_hbm.at[pl.ds(c * blocks, blocks)], corr.at[pl.ds(c * blocks, blocks)], corr_sem.at[c]
        )
        copy.start()
        corr_loads.append(copy)
    for j in range(last):
        load("basis%d" % j, basis_hbm.at[j], basis.at[j])

    def start_all(copies):
        for copy in copies:
            copy.start()
        return copies

    def remote(source, target, send_sem, recv_sem, device):
        return pltpu.make_async_remote_copy(
            src_ref=source, dst_ref=target, send_sem=send_sem, recv_sem=recv_sem,
            device_id=device, device_id_type=MESH,
        )

    for name in ("current", "weight", "route_v", "slot_v"):
        loads[name].wait()
    leaf_row = route_v[...] * LEAVES + slot_v[...]
    leaf_count = SUB * LEAVES
    hot = (
        lax.broadcasted_iota(jnp.int32, (leaf_count, PATCHES), 0)
        == jnp.broadcast_to(leaf_row, (leaf_count, PATCHES))
    ).astype(F32).astype(BF16)
    scaled_weight = weight[...] * SCALE
    for r in range(0, RHS, 2):
        pair = [
            (basis[last, pl.ds(r + i, PATCHES, stride=RHS), :] * scaled_weight).astype(BF16)
            for i in range(2)
        ]
        sums = dot(hot, jnp.concatenate(pair, axis=1))
        for t in range(SUB):
            rows = slice(t * LEAVES, (t + 1) * LEAVES)
            tile = jnp.concatenate([sums[rows, :NODES], sums[rows, NODES:]], axis=0)
            send1[t, r * LEAVES:(r + 2) * LEAVES, :] = tile.astype(BF16)

    pl.semaphore_wait(barrier, len(peers))
    copies1 = start_all([
        remote(send1.at[t], recv1.at[d], s1.at[d], r1.at[d], (w, t)) for d, t in enumerate(subs)
    ])

    loads["edge0"].wait()
    loads["edge1"].wait()
    edge_send[0] = dot(basis[last, 0:RHS, :].astype(BF16), edge_corr[0])
    edge_send[1] = dot(basis[last, ROWS - RHS:, :].astype(BF16), edge_corr[1])
    edges = start_all([
        remote(edge_send.at[0], edge_recv.at[0], edge_s.at[0], edge_r.at[0], below_id),
        remote(edge_send.at[1], edge_recv.at[1], edge_s.at[1], edge_r.at[1], above_id),
    ])

    loads["multi"].wait()
    loads["up"].wait()

    def compose_up(leaf, carry):
        high, low = split(up[leaf])
        product = dot(multi[...], high) + dot(multi[...], low)
        rows = pl.ds(pl.multiple_of(leaf * NODES, NODES), NODES)
        up_high[rows, :], up_low[rows, :] = split(product)
        return carry

    lax.fori_loop(0, LEAVES, compose_up, 0)

    def near_one(p):
        def x(q):
            return basis[last, patch_rows(q), :].astype(BF16)

        return (
            dot(x(p), corr[3 * p + 1])
            + dot(x(p + 1), corr[3 * p + 3])
            + dot(x(p - 1), corr[3 * p - 1])
        )

    def near_range(first, end):
        def body(p, carry):
            image[patch_rows(p), :] = near_one(p)
            return carry

        lax.fori_loop(first, end, body, 0)

    chunk = PATCHES // NEAR_CHUNKS

    def near_chunk(c):
        corr_loads[c].wait()
        near_range(max(1, c * chunk - 1), (c + 1) * chunk - 1)

    near_chunk(0)

    for copy in copies1:
        copy.wait_recv()
    total = send1[s].astype(F32)
    for d in range(SUB - 1):
        total = total + recv1[d].astype(F32)
    sums1[...] = total
    lanes = jnp.concatenate(
        [sums1[pl.ds(leaf, RHS, stride=LEAVES), :] for leaf in range(LEAVES)], axis=1
    )
    tree = split_dot(lanes, up_high, up_low)
    send2[0] = tree[:, :NODES]
    send2[1] = tree[:, NODES:]
    copies2 = start_all([
        remote(send2.at[t // 4], recv2.at[d], s2.at[d], r2.at[d], (w, t)) for d, t in enumerate(subs)
    ])

    loads["far"].wait()
    far_high[...], far_low[...] = split(far[...])
    near_chunk(1)
    for copy in copies1:
        copy.wait_send()

    for copy in copies2:
        copy.wait_recv()
    half = send2[s // 4]
    for d in range(SUB - 1):
        half = half + recv2[d]
    lane = lax.broadcasted_iota(jnp.int32, (RHS, NODES), 1)
    mine = jnp.where(lane // SHARE == lax.rem(s, 4), half, 0.0)
    turn = lax.rem(lax.rem(w, 4) + 4 - lax.rem(s, 4), 4)
    placed = mine
    for k in range(1, 4):
        placed = jnp.where(turn == k, pltpu.roll(mine, k * SHARE, 1), placed)
    send3[...] = placed
    copies3 = start_all([
        remote(send3, recv3.at[w], s3.at[d], r3.at[w], (v, s)) for d, v in enumerate(wides)
    ])
    recv3[w] = placed

    loads["eval"].wait()
    loads["down"].wait()

    def compose_down(leaf, carry):
        high, low = split(down[leaf])
        product = dot(high, evalm[...]) + dot(low, evalm[...])
        columns = pl.ds(pl.multiple_of(leaf * NODES, NODES), NODES)
        down_high[:, columns], down_low[:, columns] = split(product)
        return carry

    lax.fori_loop(0, LEAVES, compose_down, 0)
    near_chunk(2)
    for copy in copies2:
        copy.wait_send()

    for d, v in enumerate(wide_sources):
        remote(send3, recv3.at[v], s3.at[d], r3.at[v], (v, s)).wait_recv()
    lanes = jnp.concatenate(
        [
            (recv3[4 * g] + recv3[4 * g + 1]) + (recv3[4 * g + 2] + recv3[4 * g + 3])
            for g in range(WIDE // 4)
        ],
        axis=1,
    )
    send4[...] = split_dot(lanes, far_high, far_low)
    copies4 = start_all([
        remote(send4, recv4.at[d], s4.at[d], r4.at[d], (w, t)) for d, t in enumerate(subs)
    ])

    for j in range(last):
        loads["basis%d" % j].wait()
    zero = jnp.zeros((RHS, NODES), F32)

    def gram_body(p, sums):
        rows = patch_rows(p)
        node_weight = jnp.broadcast_to(weight[pl.ds(p, 1), :], (RHS, NODES))
        vectors = [basis[j, rows, :] for j in range(BASIS)]
        weighted = [v * node_weight for v in vectors]
        return tuple(a + weighted[j] * vectors[k] for a, (j, k) in zip(sums, PAIRS))

    gram = lax.fori_loop(0, PATCHES, gram_body, (zero,) * len(PAIRS))
    packed = zero
    for i, value in enumerate(gram):
        packed = jnp.where(lane == BASIS + 1 + i, jnp.sum(value, axis=1, keepdims=True), packed)
    for copy in copies3:
        copy.wait_send()

    for copy in copies4:
        copy.wait_recv()
    local = send4[...]
    for d in range(SUB - 1):
        local = local + recv4[d]
    potentials = split_dot(local, down_high, down_low).astype(BF16)
    for leaf in range(LEAVES):
        field[s * LEAVES + leaf] = potentials[:, leaf * NODES:(leaf + 1) * NODES]
    own = pl.ds(s * LEAVES, LEAVES)
    copies5 = start_all([
        remote(field.at[own], field.at[own], s5.at[d], r5.at[s], (w, t)) for d, t in enumerate(subs)
    ])

    near_chunk(3)
    for copy in edges:
        copy.wait()

    def current_half(p):
        return basis[last, p * RHS:(p + 1) * RHS, :].astype(BF16)

    from_below = jnp.where(me > 0, edge_recv[1], 0.0)
    from_above = jnp.where(me < WIDE * SUB - 1, edge_recv[0], 0.0)
    end = PATCHES - 1
    image[0:RHS, :] = (
        dot(current_half(0), corr[1]) + dot(current_half(1), corr[3]) + from_below
    )
    image[end * RHS:, :] = (
        dot(current_half(end), corr[3 * end + 1])
        + dot(current_half(end - 1), corr[3 * end - 1])
        + from_above
    )
    for name in ("route_s", "slot_s"):
        loads[name].wait()
    for copy in copies4:
        copy.wait_send()

    for d in range(1, SUB):
        t = lax.rem(s + SUB - d, SUB)
        block = field.at[pl.ds(t * LEAVES, LEAVES)]
        remote(block, block, s5.at[d - 1], r5.at[t], (w, t)).wait_recv()

    def products_body(p, sums):
        rows = patch_rows(p)
        leaf = route_s[0, p] * LEAVES + slot_s[0, p]
        value = image[rows, :] + field[leaf].astype(F32)
        image[rows, :] = value
        weighted = value * jnp.broadcast_to(weight[pl.ds(p, 1), :], (RHS, NODES))
        return tuple(
            a + weighted * (basis[i, rows, :] if i < BASIS else value) for i, a in enumerate(sums)
        )

    products = lax.fori_loop(0, PATCHES, products_body, (zero,) * (BASIS + 1))
    for i, value in enumerate(products):
        packed = jnp.where(lane == i, jnp.sum(value, axis=1, keepdims=True), packed)
    low_rows = RHS // 2
    send6[...] = packed[:low_rows] + pltpu.roll(packed[low_rows:], RHS, 1)
    copies6 = start_all([
        remote(send6, recv6.at[s], s6.at[d], r6.at[s], (w, t)) for d, t in enumerate(subs)
    ])
    recv6[s] = send6[...]
    for copy in copies5:
        copy.wait_send()
    for d in range(1, SUB):
        t = lax.rem(s + SUB - d, SUB)
        remote(send6, recv6.at[t], s6.at[d - 1], r6.at[t], (w, t)).wait_recv()
    total6 = recv6[0]
    for t in range(1, SUB):
        total6 = total6 + recv6[t]
    send7[...] = total6
    copies7 = start_all([
        remote(send7, recv7.at[w], s7.at[d], r7.at[w], (v, s)) for d, v in enumerate(wides)
    ])
    recv7[w] = total6
    for copy in copies6:
        copy.wait_send()
    for d, v in enumerate(wide_sources):
        remote(send7, recv7.at[v], s7.at[d], r7.at[v], (v, s)).wait_recv()
    total7 = recv7[0]
    for v in range(1, WIDE):
        total7 = total7 + recv7[v]
    total7 = total7 * (1.0 / TOTAL)
    full = jnp.concatenate([total7, pltpu.roll(total7, NODES - RHS, 1)], axis=0)

    def column(i):
        return full[:, i:i + 1]

    gram_of = {}
    for i, (j, k) in enumerate(PAIRS):
        gram_of[j, k] = gram_of[k, j] = column(BASIS + 1 + i)
    fields = [column(j) for j in range(BASIS)]
    first = [fields[j] + 0.5 * gram_of[j, last] for j in range(BASIS)]
    coeffs = []
    for j in range(BASIS):
        second = first[j]
        for k in range(BASIS):
            second = second - gram_of[j, k] * first[k]
        coeffs.append(first[j] + second)
    deltas = [coeffs[j] - 0.5 if j == last else coeffs[j] for j in range(BASIS)]
    square = column(BASIS)
    for j in range(BASIS):
        inner = -2.0 * fields[j]
        for k in range(BASIS):
            inner = inner + gram_of[j, k] * deltas[k]
        square = square + deltas[j] * inner
    beta = jnp.sqrt(jnp.maximum(square, 0.0) + 1e-6)
    inverse = jnp.broadcast_to(1.0 / beta, (RHS, NODES))
    factors = [jnp.broadcast_to(value, (RHS, NODES)) * inverse for value in deltas]

    def final_body(p, carry):
        rows = patch_rows(p)
        value = image[rows, :] * inverse
        for j in range(BASIS):
            value = value - factors[j] * basis[j, rows, :]
        vector_out[rows, :] = value
        return carry

    lax.fori_loop(0, PATCHES, final_body, 0)
    row = lax.broadcasted_iota(jnp.int32, (RHS, NODES), 0)
    columns = coeffs + [beta]
    for i, value in enumerate(columns):
        flat = jnp.sum(jnp.where(row == lane, value, 0.0), axis=0, keepdims=True)
        hess_out[i:i + 1, :] = flat[:, :RHS]
    for copy in copies7:
        copy.wait_send()


def per_device(
    krylov_basis, quad_weight, corrections, patch_route, leaf_slot, multipole_map,
    upward_translation, far_coupling, downward_translation, evaluation_map,
):
    anywhere = pl.BlockSpec(memory_space=pl.ANY)
    inside = pl.BlockSpec(memory_space=pltpu.VMEM)
    dma = pltpu.SemaphoreType.DMA
    near_blocks = 3 * PATCHES
    vector, hessenberg = pl.pallas_call(
        kernel,
        out_shape=(
            jax.ShapeDtypeStruct((ROWS, NODES), F32),
            jax.ShapeDtypeStruct((BASIS + 1, RHS), F32),
        ),
        in_specs=[anywhere] * 10,
        out_specs=(inside, inside),
        scratch_shapes=[
            pltpu.VMEM((BASIS, ROWS, NODES), F32),
            pltpu.VMEM((PATCHES, NODES), F32),
            pltpu.VMEM((near_blocks, NODES, NODES), BF16),
            pltpu.VMEM((1, PATCHES), jnp.int32),
            pltpu.VMEM((1, PATCHES), jnp.int32),
            pltpu.SMEM((1, PATCHES), jnp.int32),
            pltpu.SMEM((1, PATCHES), jnp.int32),
            pltpu.VMEM((NODES, COEFFS), BF16),
            pltpu.VMEM((LEAVES, COEFFS, COEFFS), F32),
            pltpu.VMEM((WIDE * SHARE, COEFFS), F32),
            pltpu.VMEM((LEAVES, COEFFS, COEFFS), F32),
            pltpu.VMEM((COEFFS, NODES), BF16),
            pltpu.VMEM((2, NODES, NODES), BF16),
            pltpu.VMEM((LEAVES * NODES, COEFFS), BF16),
            pltpu.VMEM((LEAVES * NODES, COEFFS), BF16),
            pltpu.VMEM((WIDE * SHARE, COEFFS), BF16),
            pltpu.VMEM((WIDE * SHARE, COEFFS), BF16),
            pltpu.VMEM((COEFFS, LEAVES * NODES), BF16),
            pltpu.VMEM((COEFFS, LEAVES * NODES), BF16),
            pltpu.VMEM((ROWS, NODES), F32),
            pltpu.VMEM((SUB, RHS * LEAVES, NODES), BF16),
            pltpu.VMEM((SUB - 1, RHS * LEAVES, NODES), BF16),
            pltpu.VMEM((RHS * LEAVES, NODES), F32),
            pltpu.VMEM((2, RHS, NODES), F32),
            pltpu.VMEM((SUB - 1, RHS, NODES), F32),
            pltpu.VMEM((RHS, NODES), F32),
            pltpu.VMEM((WIDE, RHS, NODES), F32),
            pltpu.VMEM((RHS, COEFFS), F32),
            pltpu.VMEM((SUB - 1, RHS, COEFFS), F32),
            pltpu.VMEM((SUB * LEAVES, RHS, NODES), BF16),
            pltpu.VMEM((2, RHS, NODES), F32),
            pltpu.VMEM((2, RHS, NODES), F32),
            pltpu.VMEM((RHS // 2, NODES), F32),
            pltpu.VMEM((SUB, RHS // 2, NODES), F32),
            pltpu.VMEM((RHS // 2, NODES), F32),
            pltpu.VMEM((WIDE, RHS // 2, NODES), F32),
            dma((16,)), dma((NEAR_CHUNKS,)), dma((2,)), dma((2,)),
            dma((SUB - 1,)), dma((SUB - 1,)),
            dma((SUB - 1,)), dma((SUB - 1,)),
            dma((WIDE - 1,)), dma((WIDE,)),
            dma((SUB - 1,)), dma((SUB - 1,)),
            dma((SUB - 1,)), dma((SUB,)),
            dma((SUB - 1,)), dma((SUB,)),
            dma((WIDE - 1,)), dma((WIDE,)),
        ],
        compiler_params=pltpu.CompilerParams(
            collective_id=0, has_side_effects=True, vmem_limit_bytes=40 << 20
        ),
    )(
        krylov_basis.reshape(BASIS, ROWS, NODES),
        quad_weight,
        corrections.reshape(near_blocks, NODES, NODES),
        patch_route.reshape(1, PATCHES),
        leaf_slot.reshape(1, PATCHES),
        multipole_map,
        upward_translation,
        far_coupling.reshape(WIDE * SHARE, COEFFS),
        downward_translation,
        evaluation_map,
    )
    return vector.reshape(PATCHES, RHS, NODES), hessenberg


def solution(mesh):
    return jax.shard_map(
        per_device,
        mesh=mesh,
        in_specs=(
            P(None, ("wide", "sub"), None, None),
            P(("wide", "sub"), None),
            P(("wide", "sub"), None, None, None),
            P(("wide", "sub"), None),
            P(("wide", "sub")),
            P(),
            P(("wide", "sub"), None, None),
            P("wide", None, "sub", None),
            P(("wide", "sub"), None, None),
            P(),
        ),
        out_specs=(P(("wide", "sub"), None, None), P()),
        check_vma=False,
    )
```

time: 479 us -> 61.1 us (0.13); the launches traced: 469 us -> 60.6 us
  blocking collectives: 238 us -> 0 us
  matrix products: 105 us -> 0 us
  waiting for transfers between devices: 67.6 us -> 0 us
  Pallas kernels: 0 us -> 48.2 us
  starting transfers between devices: 25.2 us -> 0 us
  between operations: 14.5 us -> 0.66 us
  other arithmetic: 12 us -> 0 us
  local copies, waits for them, and re-layouts: 6.27 us -> 11.8 us
    psum x4 -> x0, blocking collectives: 219 us -> none  [the longest x1 64.1 us: per_device(): lax.psum(weighted_products(krylov_basis, operator_out, quad_weight, total...]
    dot_general x15 -> x0, matrix products: 105 us -> none  [the longest x2 55 us: weighted_products(): jnp.einsum('jprq,prq,pq->jr', basis_set, vector, weights, precision=HIGHEST)]
    pallas_call x0 -> x1, Pallas kernels: none -> 48.2 us  [per_device(): pl.pallas_call(kernel, out_shape=(jax.ShapeDtypeStruct((ROWS, NODES), F32...]
    all_to_all x3 -> x0, waiting for transfers between devices: 40 us -> none  [the longest x1 26.4 us: per_device(): lax.all_to_all(packed.reshape(sub_count, capacity, rhs_count * node_count...]
    unnamed x2 -> x0, waiting for transfers between devices: 27.5 us -> none
    all_to_all x3 -> x0, starting transfers between devices: 19.6 us -> none  [the longest x1 7.77 us: per_device(): lax.all_to_all(slot_field.reshape(sub_count, capacity, rhs_count * node_c...]
    all_gather x1 -> x0, blocking collectives: 18.7 us -> none  [per_device(): all_trees = lax.all_gather(tree_share[None], 'wide', axis=0, tiled=True)]
    unnamed x31 -> x20, local copies, waits for them, and re-layouts: 3.17 us -> 11.8 us
  transfers between devices with their start and end apart: 6 -> 0, of which waited for: 4 -> 0; matrix products, arithmetic and copies ran while one was open for 3% -> 0% of each run, Pallas kernels for 0% -> 0%
where the time goes in v1:
time: 61.1 us; the launch traced here: 60.6 us
  Pallas kernels  48.2 us (79%)
  local copies, waits for them, and re-layouts  11.8 us (19%)
  between operations  0.66 us (1%)
    pallas_call x1, Pallas kernels, per_device(): pl.pallas_call(kernel, out_shape=(jax.ShapeDtypeStruct((ROWS, NODES), F32...  48.2 us
    unnamed x20, local copies, waits for them, and re-layouts  11.8 us

profile of v1, /device:TPU:1, one launch (start us, length us, event | category | flops | bytes accessed | tf_op | source)
XLA Modules:
  0.0 60.6 jit_solution(11767952244415343435)
XLA Ops:
  0.6 0.0 copy-start
  0.6 2.2 %copy-done = f32[4,128,16,128]{3,2,1,0:T(8,128)S(1)} copy-done((f32[4,128,16,128]{3,2,1,0:T(8,128)S(1)}, f32[4,128,16,128]{3,2,1,0:T(8,128)}, u32[]{:S(2)}) %copy-start) | copy-done | bytes 4194328
  2.8 0.0 copy-start.1
  2.8 1.6 %copy-done.1 = f32[8,256,256]{2,1,0:T(8,128)S(1)} copy-done((f32[8,256,256]{2,1,0:T(8,128)S(1)}, f32[8,256,256]{2,1,0:T(8,128)}, u32[]{:S(2)}) %copy-start.1) | copy-done | bytes 2097176
  4.4 0.0 copy-start.2
  4.4 1.6 %copy-done.2 = f32[8,256,256]{2,1,0:T(8,128)S(1)} copy-done((f32[8,256,256]{2,1,0:T(8,128)S(1)}, f32[8,256,256]{2,1,0:T(8,128)}, u32[]{:S(2)}) %copy-start.2) | copy-done | bytes 2097176
  6.0 0.0 copy-start.3
  6.0 1.0 %copy-done.3 = f32[1,16,32,256]{3,2,1,0:T(8,128)S(1)} copy-done((f32[1,16,32,256]{3,2,1,0:T(8,128)S(1)}, f32[1,16,32,256]{3,2,1,0:T(8,128)}, u32[]{:S(2)}) %copy-start.3) | copy-done | bytes 524312
  7.0 0.0 copy-start.4
  7.0 0.8 %copy-done.4 = f32[128,128]{1,0:T(8,128)S(1)} copy-done((f32[128,128]{1,0:T(8,128)S(1)}, f32[128,128]{1,0:T(8,128)}, u32[]{:S(2)}) %copy-start.4) | copy-done | bytes 65560
  7.9 0.0 copy-start.5
  7.9 0.8 %copy-done.5 = bf16[128,256]{1,0:T(8,128)(2,1)S(1)} copy-done((bf16[128,256]{1,0:T(8,128)(2,1)S(1)}, bf16[128,256]{1,0:T(8,128)(2,1)}, u32[]{:S(2)}) %copy-start.5) | copy-done | bytes 65560
  8.7 0.0 copy-start.6
  8.7 0.8 %copy-done.6 = bf16[256,128]{1,0:T(8,128)(2,1)S(1)} copy-done((bf16[256,128]{1,0:T(8,128)(2,1)S(1)}, bf16[256,128]{1,0:T(8,128)(2,1)}, u32[]{:S(2)}) %copy-start.6) | copy-done | bytes 65560
  9.6 0.0 copy-start.7
  9.6 0.7 %copy-done.7 = s32[128,1]{0,1:T(1,128)S(1)} copy-done((s32[128,1]{0,1:T(1,128)S(1)}, s32[128,1]{0,1:T(1,128)}, u32[]{:S(2)}) %copy-start.7) | copy-done | bytes 536
  10.2 0.0 copy-start.8
  10.2 0.7 %copy-done.8 = s32[128]{0:T(128)S(1)} copy-done((s32[128]{0:T(128)S(1)}, s32[128]{0:T(128)}, u32[]{:S(2)}) %copy-start.8) | copy-done | bytes 536
  10.9 48.2 %shard_map.113 = (f32[2048,128]{1,0:T(8,128)S(1)}, f32[5,16]{1,0:T(8,128)S(1)}) custom-call(f32[4,2048,128]{2,1,0:T(8,128)S(1)} %bitcast.6, f32[128,128]{1,0:T(8,128)S(1)} %copy-done.4, bf16[384,128,128]{2,1,0:T(8,128)(2,1)} %bitcast.11, s32[1,128]{1,0:T(1,128)S(1)} %bitcast.9, s32[1,128]{1,0:T(1,128)S(1)} %bitcast.10, bf16[128,256]{1,0:T(8,128)(2,1)S(1)} %copy-done.5, ...), custom_call_target="tpu_custom_call" | custom-call | tf_op jit(solution)/shard_map/pallas_call | solution.py:402
  59.1 1.0 %copy.14 = f32[128,16,128]{2,1,0:T(8,128)} copy(f32[128,16,128]{2,1,0:T(8,128)S(1)} %bitcast.7) | data formatting | bytes 2097152
  60.0 0.6 copy.15
Async XLA Ops:
  0.6 2.2 %copy-start = (f32[4,128,16,128]{3,2,1,0:T(8,128)S(1)}, f32[4,128,16,128]{3,2,1,0:T(8,128)}, u32[]{:S(2)}) copy-start(f32[4,128,16,128]{3,2,1,0:T(8,128)} %param.10) | copy-start | bytes 12582916
  2.8 1.6 %copy-start.1 = (f32[8,256,256]{2,1,0:T(8,128)S(1)}, f32[8,256,256]{2,1,0:T(8,128)}, u32[]{:S(2)}) copy-start(f32[8,256,256]{2,1,0:T(8,128)} %up_hbm.1) | copy-start | bytes 6291460
  4.4 1.6 %copy-start.2 = (f32[8,256,256]{2,1,0:T(8,128)S(1)}, f32[8,256,256]{2,1,0:T(8,128)}, u32[]{:S(2)}) copy-start(f32[8,256,256]{2,1,0:T(8,128)} %down_hbm.1) | copy-start | bytes 6291460
  6.0 1.0 %copy-start.3 = (f32[1,16,32,256]{3,2,1,0:T(8,128)S(1)}, f32[1,16,32,256]{3,2,1,0:T(8,128)}, u32[]{:S(2)}) copy-start(f32[1,16,32,256]{3,2,1,0:T(8,128)} %param.17) | copy-start | bytes 1572868
  7.0 0.8 %copy-start.4 = (f32[128,128]{1,0:T(8,128)S(1)}, f32[128,128]{1,0:T(8,128)}, u32[]{:S(2)}) copy-start(f32[128,128]{1,0:T(8,128)} %weight_hbm.1) | copy-start | bytes 196612
  7.9 0.8 %copy-start.5 = (bf16[128,256]{1,0:T(8,128)(2,1)S(1)}, bf16[128,256]{1,0:T(8,128)(2,1)}, u32[]{:S(2)}) copy-start(bf16[128,256]{1,0:T(8,128)(2,1)} %multi_hbm.1) | copy-start | bytes 196612
  8.7 0.8 %copy-start.6 = (bf16[256,128]{1,0:T(8,128)(2,1)S(1)}, bf16[256,128]{1,0:T(8,128)(2,1)}, u32[]{:S(2)}) copy-start(bf16[256,128]{1,0:T(8,128)(2,1)} %eval_hbm.1) | copy-start | bytes 196612
  9.6 0.7 %copy-start.7 = (s32[128,1]{0,1:T(1,128)S(1)}, s32[128,1]{0,1:T(1,128)}, u32[]{:S(2)}) copy-start(s32[128,1]{0,1:T(1,128)} %param.13) | copy-start | bytes 1540
  10.2 0.7 %copy-start.8 = (s32[128]{0:T(128)S(1)}, s32[128]{0:T(128)}, u32[]{:S(2)}) copy-start(s32[128]{0:T(128)} %param.14) | copy-start | bytes 1540

commit v2 on v1

--- a/solution.py
+++ b/solution.py
@@ -46,8 +46,9 @@
     basis, weight, corr, route_v, slot_v, route_s, slot_s, multi, up, far, down, evalm, edge_corr,
     up_high, up_low, far_high, far_low, down_high, down_low, image,
     send1, recv1, sums1, send2, recv2, send3, recv3, send4, recv4, field,
-    edge_send, edge_recv, send6, recv6, send7, recv7,
+    edge_send, edge_recv, send6, recv6, send7, recv7, bulk_send, bulk_recv, bulk_sums, area_send, area_recv,
     load_sem, corr_sem, edge_s, edge_r, s1, r1, s2, r2, s3, r3, s4, r4, s5, r5, s6, r6, s7, r7,
+    s8, r8, s9, r9, s10, r10,
 ):
     w = lax.axis_index("wide")
     s = lax.axis_index("sub")
@@ -81,11 +82,9 @@
     load("up", up_hbm, up)
     load("edge0", corr_hbm.at[0], edge_corr.at[0])
     load("edge1", corr_hbm.at[3 * PATCHES - 1], edge_corr.at[1])
+    load("basis", basis_hbm.at[pl.ds(0, last)], basis.at[pl.ds(0, last)])
     load("route_s", route_hbm, route_s)
     load("slot_s", slot_hbm, slot_s)
-    load("far", far_hbm, far)
-    load("eval", eval_hbm, evalm)
-    load("down", down_hbm, down)
     blocks = 3 * PATCHES // NEAR_CHUNKS
     corr_loads = []
     for c in range(NEAR_CHUNKS):
@@ -94,8 +93,9 @@
         )
         copy.start()
         corr_loads.append(copy)
-    for j in range(last):
-        load("basis%d" % j, basis_hbm.at[j], basis.at[j])
+    load("far", far_hbm, far)
+    load("eval", eval_hbm, evalm)
+    load("down", down_hbm, down)
 
     def start_all(copies):
         for copy in copies:
@@ -117,16 +117,20 @@
         == jnp.broadcast_to(leaf_row, (leaf_count, PATCHES))
     ).astype(F32).astype(BF16)
     scaled_weight = weight[...] * SCALE
-    for r in range(0, RHS, 2):
-        pair = [
-            (basis[last, pl.ds(r + i, PATCHES, stride=RHS), :] * scaled_weight).astype(BF16)
-            for i in range(2)
-        ]
-        sums = dot(hot, jnp.concatenate(pair, axis=1))
-        for t in range(SUB):
-            rows = slice(t * LEAVES, (t + 1) * LEAVES)
-            tile = jnp.concatenate([sums[rows, :NODES], sums[rows, NODES:]], axis=0)
-            send1[t, r * LEAVES:(r + 2) * LEAVES, :] = tile.astype(BF16)
+
+    def leaf_sums(read, store):
+        for r in range(0, RHS, 2):
+            pair = [(read(pl.ds(r + i, PATCHES, stride=RHS)) * scaled_weight).astype(BF16) for i in range(2)]
+            sums = dot(hot, jnp.concatenate(pair, axis=1))
+            for t in range(SUB):
+                rows = slice(t * LEAVES, (t + 1) * LEAVES)
+                tile = jnp.concatenate([sums[rows, :NODES], sums[rows, NODES:]], axis=0)
+                store(t, slice(r * LEAVES, (r + 2) * LEAVES), tile.astype(BF16))
+
+    def store1(t, rows, tile):
+        send1[t, rows, :] = tile
+
+    leaf_sums(lambda rows: basis[last, rows, :], store1)
 
     pl.semaphore_wait(barrier, len(peers))
     copies1 = start_all([
@@ -154,30 +158,45 @@
 
     lax.fori_loop(0, LEAVES, compose_up, 0)
 
-    def near_one(p):
-        def x(q):
-            return basis[last, patch_rows(q), :].astype(BF16)
-
-        return (
-            dot(x(p), corr[3 * p + 1])
-            + dot(x(p + 1), corr[3 * p + 3])
-            + dot(x(p - 1), corr[3 * p - 1])
+    def half(p):
+        return basis[last, patch_rows(p), :].astype(BF16)
+
+    def near_pair(h, carry):
+        p = 2 * h + 1
+        left = jnp.concatenate([half(p), half(p + 1)], axis=1)
+        right = jnp.concatenate(
+            [
+                jnp.concatenate([corr[3 * p + 1], corr[3 * p + 2]], axis=1),
+                jnp.concatenate([corr[3 * p + 3], corr[3 * p + 4]], axis=1),
+            ],
+            axis=0,
         )
-
-    def near_range(first, end):
-        def body(p, carry):
-            image[patch_rows(p), :] = near_one(p)
-            return carry
-
-        lax.fori_loop(first, end, body, 0)
-
-    chunk = PATCHES // NEAR_CHUNKS
+        both = dot(left, right)
+        image[patch_rows(p), :] = both[:, :NODES] + dot(half(p - 1), corr[3 * p - 1])
+        image[patch_rows(p + 1), :] = both[:, NODES:] + dot(half(p + 2), corr[3 * p + 6])
+        return carry
+
+    chunk = PATCHES // NEAR_CHUNKS // 2
 
     def near_chunk(c):
         corr_loads[c].wait()
-        near_range(max(1, c * chunk - 1), (c + 1) * chunk - 1)
-
+        lax.fori_loop(max(0, c * chunk - 1), (c + 1) * chunk - 1, near_pair, 0, unroll=5 if c == 0 else 8)
+
+    def bulk_store(j):
+        def store(t, rows, tile):
+            bulk_send[t, j, rows, :] = tile
+
+        return store
+
+    loads["basis"].wait()
+    for j in range(last):
+        leaf_sums(functools.partial(lambda k, rows: basis[k, rows, :], j), bulk_store(j))
+    area_high, area_low = split(weight[...])
+    areas = dot(hot, area_high) + dot(hot, area_low)
+    for t in range(SUB):
+        area_send[t] = areas[t * LEAVES:(t + 1) * LEAVES]
     near_chunk(0)
+    near_chunk(1)
 
     for copy in copies1:
         copy.wait_recv()
@@ -195,19 +214,44 @@
         remote(send2.at[t // 4], recv2.at[d], s2.at[d], r2.at[d], (w, t)) for d, t in enumerate(subs)
     ])
 
+    copies8 = start_all([
+        remote(bulk_send.at[t, pl.ds(0, last)], bulk_recv.at[d, pl.ds(0, last)], s8.at[d], r8.at[d], (w, t))
+        for d, t in enumerate(subs)
+    ] + [
+        remote(area_send.at[t], area_recv.at[d], s9.at[d], r9.at[d], (w, t)) for d, t in enumerate(subs)
+    ])
+
     loads["far"].wait()
     far_high[...], far_low[...] = split(far[...])
-    near_chunk(1)
+    near_chunk(2)
+    near_chunk(3)
+    for copy in edges:
+        copy.wait()
+
+    def current_half(p):
+        return basis[last, p * RHS:(p + 1) * RHS, :].astype(BF16)
+
+    from_below = jnp.where(me > 0, edge_recv[1], 0.0)
+    from_above = jnp.where(me < WIDE * SUB - 1, edge_recv[0], 0.0)
+    end = PATCHES - 1
+    image[0:RHS, :] = (
+        dot(current_half(0), corr[1]) + dot(current_half(1), corr[3]) + from_below
+    )
+    image[end * RHS:, :] = (
+        dot(current_half(end), corr[3 * end + 1])
+        + dot(current_half(end - 1), corr[3 * end - 1])
+        + from_above
+    )
     for copy in copies1:
         copy.wait_send()
 
     for copy in copies2:
         copy.wait_recv()
-    half = send2[s // 4]
+    half_tree = send2[s // 4]
     for d in range(SUB - 1):
-        half = half + recv2[d]
+        half_tree = half_tree + recv2[d]
     lane = lax.broadcasted_iota(jnp.int32, (RHS, NODES), 1)
-    mine = jnp.where(lane // SHARE == lax.rem(s, 4), half, 0.0)
+    mine = jnp.where(lane // SHARE == lax.rem(s, 4), half_tree, 0.0)
     turn = lax.rem(lax.rem(w, 4) + 4 - lax.rem(s, 4), 4)
     placed = mine
     for k in range(1, 4):
@@ -218,6 +262,12 @@
     ])
     recv3[w] = placed
 
+    leaf_sums(lambda rows: image[rows, :], bulk_store(last))
+    copies10 = start_all([
+        remote(bulk_send.at[t, last], bulk_recv.at[d, last], s10.at[d], r10.at[d], (w, t))
+        for d, t in enumerate(subs)
+    ])
+
     loads["eval"].wait()
     loads["down"].wait()
 
@@ -229,7 +279,21 @@
         return carry
 
     lax.fori_loop(0, LEAVES, compose_down, 0)
-    near_chunk(2)
+    zero = jnp.zeros((RHS, NODES), F32)
+
+    def node_weight(p):
+        return jnp.broadcast_to(weight[pl.ds(p, 1), :], (RHS, NODES))
+
+    def gram_body(p, sums):
+        rows = patch_rows(p)
+        vectors = [basis[j, rows, :] for j in range(BASIS)]
+        weighted = [v * node_weight(p) for v in vectors]
+        return tuple(a + weighted[j] * vectors[k] for a, (j, k) in zip(sums, PAIRS))
+
+    gram = lax.fori_loop(0, PATCHES, gram_body, (zero,) * len(PAIRS), unroll=2)
+    packed = zero
+    for i, value in enumerate(gram):
+        packed = jnp.where(lane == BASIS + 1 + i, jnp.sum(value, axis=1, keepdims=True), packed)
     for copy in copies2:
         copy.wait_send()
 
@@ -247,23 +311,27 @@
         remote(send4, recv4.at[d], s4.at[d], r4.at[d], (w, t)) for d, t in enumerate(subs)
     ])
 
-    for j in range(last):
-        loads["basis%d" % j].wait()
-    zero = jnp.zeros((RHS, NODES), F32)
-
-    def gram_body(p, sums):
+    def near_products(p, sums):
         rows = patch_rows(p)
-        node_weight = jnp.broadcast_to(weight[pl.ds(p, 1), :], (RHS, NODES))
-        vectors = [basis[j, rows, :] for j in range(BASIS)]
-        weighted = [v * node_weight for v in vectors]
-        return tuple(a + weighted[j] * vectors[k] for a, (j, k) in zip(sums, PAIRS))
-
-    gram = lax.fori_loop(0, PATCHES, gram_body, (zero,) * len(PAIRS))
-    packed = zero
-    for i, value in enumerate(gram):
-        packed = jnp.where(lane == BASIS + 1 + i, jnp.sum(value, axis=1, keepdims=True), packed)
+        value = image[rows, :]
+        weighted = value * node_weight(p)
+        return tuple(
+            a + weighted * (basis[i, rows, :] if i < BASIS else value) for i, a in enumerate(sums)
+        )
+
+    products = lax.fori_loop(0, PATCHES, near_products, (zero,) * (BASIS + 1), unroll=2)
     for copy in copies3:
         copy.wait_send()
+    for copy in copies8 + copies10:
+        copy.wait_recv()
+    for j in range(BASIS):
+        total = bulk_send[s, j].astype(F32)
+        for d in range(SUB - 1):
+            total = total + bulk_recv[d, j].astype(F32)
+        bulk_sums[j] = total
+    area = area_send[s]
+    for d in range(SUB - 1):
+        area = area + area_recv[d]
 
     for copy in copies4:
         copy.wait_recv()
@@ -271,80 +339,67 @@
     for d in range(SUB - 1):
         local = local + recv4[d]
     potentials = split_dot(local, down_high, down_low).astype(BF16)
+    far_sums = [zero] * (BASIS + 2)
     for leaf in range(LEAVES):
         field[s * LEAVES + leaf] = potentials[:, leaf * NODES:(leaf + 1) * NODES]
+        value = potentials[:, leaf * NODES:(leaf + 1) * NODES].astype(F32)
+        rows = pl.ds(leaf, RHS, stride=LEAVES)
+        others = [bulk_sums[j, rows, :] for j in range(last)]
+        others += [sums1[rows, :], bulk_sums[last, rows, :]]
+        others += [value * jnp.broadcast_to(area[leaf:leaf + 1], (RHS, NODES))]
+        far_sums = [a + value * b for a, b in zip(far_sums, others)]
+    products = [products[j] + far_sums[j] * (1.0 / SCALE) for j in range(BASIS)] + [
+        products[BASIS] + far_sums[BASIS] * (2.0 / SCALE) + far_sums[BASIS + 1]
+    ]
+    for i, value in enumerate(products):
+        packed = jnp.where(lane == i, jnp.sum(value, axis=1, keepdims=True), packed)
+    low_rows = RHS // 2
+    share = packed[:low_rows] + pltpu.roll(packed[low_rows:], RHS, 1)
+    send7[...] = share
+    copies7 = start_all([
+        remote(send7, recv7.at[w], s7.at[d], r7.at[w], (v, s)) for d, v in enumerate(wides)
+    ])
+    recv7[w] = share
     own = pl.ds(s * LEAVES, LEAVES)
     copies5 = start_all([
         remote(field.at[own], field.at[own], s5.at[d], r5.at[s], (w, t)) for d, t in enumerate(subs)
     ])
-
-    near_chunk(3)
-    for copy in edges:
-        copy.wait()
-
-    def current_half(p):
-        return basis[last, p * RHS:(p + 1) * RHS, :].astype(BF16)
-
-    from_below = jnp.where(me > 0, edge_recv[1], 0.0)
-    from_above = jnp.where(me < WIDE * SUB - 1, edge_recv[0], 0.0)
-    end = PATCHES - 1
-    image[0:RHS, :] = (
-        dot(current_half(0), corr[1]) + dot(current_half(1), corr[3]) + from_below
-    )
-    image[end * RHS:, :] = (
-        dot(current_half(end), corr[3 * end + 1])
-        + dot(current_half(end - 1), corr[3 * end - 1])
-        + from_above
-    )
     for name in ("route_s", "slot_s"):
         loads[name].wait()
-    for copy in copies4:
+    for copy in copies4 + copies8 + copies10:
         copy.wait_send()
 
-    for d in range(1, SUB):
-        t = lax.rem(s + SUB - d, SUB)
-        block = field.at[pl.ds(t * LEAVES, LEAVES)]
-        remote(block, block, s5.at[d - 1], r5.at[t], (w, t)).wait_recv()
-
-    def products_body(p, sums):
-        rows = patch_rows(p)
-        leaf = route_s[0, p] * LEAVES + slot_s[0, p]
-        value = image[rows, :] + field[leaf].astype(F32)
-        image[rows, :] = value
-        weighted = value * jnp.broadcast_to(weight[pl.ds(p, 1), :], (RHS, NODES))
-        return tuple(
-            a + weighted * (basis[i, rows, :] if i < BASIS else value) for i, a in enumerate(sums)
-        )
-
-    products = lax.fori_loop(0, PATCHES, products_body, (zero,) * (BASIS + 1))
-    for i, value in enumerate(products):
-        packed = jnp.where(lane == i, jnp.sum(value, axis=1, keepdims=True), packed)
-    low_rows = RHS // 2
-    send6[...] = packed[:low_rows] + pltpu.roll(packed[low_rows:], RHS, 1)
-    copies6 = start_all([
-        remote(send6, recv6.at[s], s6.at[d], r6.at[s], (w, t)) for d, t in enumerate(subs)
-    ])
-    recv6[s] = send6[...]
-    for copy in copies5:
-        copy.wait_send()
-    for d in range(1, SUB):
-        t = lax.rem(s + SUB - d, SUB)
-        remote(send6, recv6.at[t], s6.at[d - 1], r6.at[t], (w, t)).wait_recv()
-    total6 = recv6[0]
-    for t in range(1, SUB):
-        total6 = total6 + recv6[t]
-    send7[...] = total6
-    copies7 = start_all([
-        remote(send7, recv7.at[w], s7.at[d], r7.at[w], (v, s)) for d, v in enumerate(wides)
-    ])
-    recv7[w] = total6
-    for copy in copies6:
-        copy.wait_send()
     for d, v in enumerate(wide_sources):
         remote(send7, recv7.at[v], s7.at[d], r7.at[v], (v, s)).wait_recv()
     total7 = recv7[0]
     for v in range(1, WIDE):
         total7 = total7 + recv7[v]
+    send6[...] = total7
+    copies6 = start_all([
+        remote(send6, recv6.at[s], s6.at[d], r6.at[s], (w, t)) for d, t in enumerate(subs)
+    ])
+    recv6[s] = total7
+
+    for d in range(1, SUB):
+        t = lax.rem(s + SUB - d, SUB)
+        block = field.at[pl.ds(t * LEAVES, LEAVES)]
+        remote(block, block, s5.at[d - 1], r5.at[t], (w, t)).wait_recv()
+
+    def add_far(p, carry):
+        rows = patch_rows(p)
+        leaf = route_s[0, p] * LEAVES + slot_s[0, p]
+        image[rows, :] = image[rows, :] + field[leaf].astype(F32)
+        return carry
+
+    lax.fori_loop(0, PATCHES, add_far, 0, unroll=4)
+    for copy in copies5 + copies7:
+        copy.wait_send()
+    for d in range(1, SUB):
+        t = lax.rem(s + SUB - d, SUB)
+        remote(send6, recv6.at[t], s6.at[d - 1], r6.at[t], (w, t)).wait_recv()
+    total7 = recv6[0]
+    for t in range(1, SUB):
+        total7 = total7 + recv6[t]
     total7 = total7 * (1.0 / TOTAL)
     full = jnp.concatenate([total7, pltpu.roll(total7, NODES - RHS, 1)], axis=0)
 
@@ -381,13 +436,13 @@
         vector_out[rows, :] = value
         return carry
 
-    lax.fori_loop(0, PATCHES, final_body, 0)
+    lax.fori_loop(0, PATCHES, final_body, 0, unroll=4)
     row = lax.broadcasted_iota(jnp.int32, (RHS, NODES), 0)
     columns = coeffs + [beta]
     for i, value in enumerate(columns):
         flat = jnp.sum(jnp.where(row == lane, value, 0.0), axis=0, keepdims=True)
         hess_out[i:i + 1, :] = flat[:, :RHS]
-    for copy in copies7:
+    for copy in copies6:
         copy.wait_send()
 
 
@@ -395,7 +450,7 @@
     krylov_basis, quad_weight, corrections, patch_route, leaf_slot, multipole_map,
     upward_translation, far_coupling, downward_translation, evaluation_map,
 ):
-    anywhere = pl.BlockSpec(memory_space=pl.ANY)
+    outside = pl.BlockSpec(memory_space=pl.ANY)
     inside = pl.BlockSpec(memory_space=pltpu.VMEM)
     dma = pltpu.SemaphoreType.DMA
     near_blocks = 3 * PATCHES
@@ -405,7 +460,7 @@
             jax.ShapeDtypeStruct((ROWS, NODES), F32),
             jax.ShapeDtypeStruct((BASIS + 1, RHS), F32),
         ),
-        in_specs=[anywhere] * 10,
+        in_specs=[outside] * 10,
         out_specs=(inside, inside),
         scratch_shapes=[
             pltpu.VMEM((BASIS, ROWS, NODES), F32),
@@ -444,6 +499,11 @@
             pltpu.VMEM((SUB, RHS // 2, NODES), F32),
             pltpu.VMEM((RHS // 2, NODES), F32),
             pltpu.VMEM((WIDE, RHS // 2, NODES), F32),
+            pltpu.VMEM((SUB, BASIS, RHS * LEAVES, NODES), BF16),
+            pltpu.VMEM((SUB - 1, BASIS, RHS * LEAVES, NODES), BF16),
+            pltpu.VMEM((BASIS, RHS * LEAVES, NODES), F32),
+            pltpu.VMEM((SUB, LEAVES, NODES), F32),
+            pltpu.VMEM((SUB - 1, LEAVES, NODES), F32),
             dma((16,)), dma((NEAR_CHUNKS,)), dma((2,)), dma((2,)),
             dma((SUB - 1,)), dma((SUB - 1,)),
             dma((SUB - 1,)), dma((SUB - 1,)),
@@ -452,9 +512,12 @@
             dma((SUB - 1,)), dma((SUB,)),
             dma((SUB - 1,)), dma((SUB,)),
             dma((WIDE - 1,)), dma((WIDE,)),
+            dma((SUB - 1,)), dma((SUB - 1,)),
+            dma((SUB - 1,)), dma((SUB - 1,)),
+            dma((SUB - 1,)), dma((SUB - 1,)),
         ],
         compiler_params=pltpu.CompilerParams(
-            collective_id=0, has_side_effects=True, vmem_limit_bytes=40 << 20
+            collective_id=0, has_side_effects=True, vmem_limit_bytes=60 << 20
         ),
     )(
         krylov_basis.reshape(BASIS, ROWS, NODES),

time: 61.1 us -> 47.6 us (0.78)
  local copies, waits for them, and re-layouts: 11.8 us -> 3.53 us
  Pallas kernels: 48.2 us -> 43.3 us
    unnamed x20 -> x2, local copies, waits for them, and re-layouts: 11.8 us -> 3.53 us
    pallas_call x1, Pallas kernels: 48.2 us -> 43.3 us  [per_device(): pl.pallas_call(kernel, out_shape=(jax.ShapeDtypeStruct((ROWS, NODES), F32...]
where the time goes in v2:
time: 47.6 us; the launch traced here: 47.5 us
  Pallas kernels  43.3 us (91%)
  local copies, waits for them, and re-layouts  3.53 us (7%)
  between operations  0.64 us (1%)
    pallas_call x1, Pallas kernels, per_device(): pl.pallas_call(kernel, out_shape=(jax.ShapeDtypeStruct((ROWS, NODES), F32...  43.3 us
    unnamed x2, local copies, waits for them, and re-layouts  3.53 us

profile of v2, /device:TPU:1, one launch (start us, length us, event | category | flops | bytes accessed | tf_op | source)
XLA Modules:
  0.0 47.5 jit_solution(1181403178417858085)
XLA Ops:
  0.6 43.3 %shard_map.113 = (f32[2048,128]{1,0:T(8,128)}, f32[5,16]{1,0:T(8,128)}) custom-call(f32[4,2048,128]{2,1,0:T(8,128)} %bitcast.7, f32[128,128]{1,0:T(8,128)} %weight_hbm.1, bf16[384,128,128]{2,1,0:T(8,128)(2,1)} %bitcast.6, s32[1,128]{1,0:T(1,128)} %bitcast.10, s32[1,128]{1,0:T(1,128)} %bitcast.11, bf16[128,256]{1,0:T(8,128)(2,1)} %multi_hbm.1, ...), custom_call_target="tpu_custom_call" | custom-call | tf_op jit(solution)/shard_map/pallas_call | solution.py:457
  43.9 2.3 %copy.14 = f32[128,16,128]{2,1,0:T(8,128)} copy(f32[128,16,128]{2,1,0:T(8,128)} %bitcast.8) | data formatting | bytes 2097152
  46.2 1.3 %copy.15 = f32[5,16]{1,0:T(8,128)} copy(f32[5,16]{1,0:T(8,128)} %get-tuple-element.9) | data formatting | bytes 640

commit v3 on v2

--- a/solution.py
+++ b/solution.py
@@ -46,9 +46,9 @@
     basis, weight, corr, route_v, slot_v, route_s, slot_s, multi, up, far, down, evalm, edge_corr,
     up_high, up_low, far_high, far_low, down_high, down_low, image,
     send1, recv1, sums1, send2, recv2, send3, recv3, send4, recv4, field,
-    edge_send, edge_recv, send6, recv6, send7, recv7, bulk_send, bulk_recv, bulk_sums, area_send, area_recv,
+    edge_send, edge_recv, send6, recv6, send7, recv7, bulk_send, pair_recv, pair_sums, bulk_recv, bulk_sums, area_send, area_recv,
     load_sem, corr_sem, edge_s, edge_r, s1, r1, s2, r2, s3, r3, s4, r4, s5, r5, s6, r6, s7, r7,
-    s8, r8, s9, r9, s10, r10,
+    s8, r8, s9, r9, s10, r10, pair_s, pair_r,
 ):
     w = lax.axis_index("wide")
     s = lax.axis_index("sub")
@@ -58,6 +58,9 @@
     below_id = (below // SUB, lax.rem(below, SUB))
     above_id = (above // SUB, lax.rem(above, SUB))
     subs = [lax.rem(s + d, SUB) for d in range(1, SUB)]
+    core = lax.rem(s, 2)
+    sibling = (w, s + 1 - 2 * core)
+    columns_z = [(lax.rem(s // 2 + d, SUB // 2), d - 1) for d in range(1, SUB // 2)]
     wides = [lax.rem(w + d, WIDE) for d in range(1, WIDE)]
     wide_sources = [lax.rem(w + WIDE - d, WIDE) for d in range(1, WIDE)]
 
@@ -184,7 +187,7 @@
 
     def bulk_store(j):
         def store(t, rows, tile):
-            bulk_send[t, j, rows, :] = tile
+            bulk_send[t % 2, t // 2, j, rows, :] = tile
 
         return store
 
@@ -195,6 +198,11 @@
     areas = dot(hot, area_high) + dot(hot, area_low)
     for t in range(SUB):
         area_send[t] = areas[t * LEAVES:(t + 1) * LEAVES]
+    early = pl.ds(0, last)
+    pair_early = remote(
+        bulk_send.at[1 - core, :, early], pair_recv.at[:, early], pair_s.at[0], pair_r.at[0], sibling
+    )
+    pair_early.start()
     near_chunk(0)
     near_chunk(1)
 
@@ -214,9 +222,19 @@
         remote(send2.at[t // 4], recv2.at[d], s2.at[d], r2.at[d], (w, t)) for d, t in enumerate(subs)
     ])
 
+    def pair_add(j):
+        for t in range(SUB // 2):
+            both = bulk_send[core, t, j].astype(F32) + pair_recv[t, j].astype(F32)
+            pair_sums[t, j] = both.astype(BF16)
+
+    pair_early.wait_recv()
+    for j in range(last):
+        pair_add(j)
     copies8 = start_all([
-        remote(bulk_send.at[t, pl.ds(0, last)], bulk_recv.at[d, pl.ds(0, last)], s8.at[d], r8.at[d], (w, t))
-        for d, t in enumerate(subs)
+        remote(
+            pair_sums.at[t, early], bulk_recv.at[d, early], s8.at[d], r8.at[d], (w, 2 * t + core)
+        )
+        for t, d in columns_z
     ] + [
         remote(area_send.at[t], area_recv.at[d], s9.at[d], r9.at[d], (w, t)) for d, t in enumerate(subs)
     ])
@@ -242,6 +260,11 @@
         + dot(current_half(end - 1), corr[3 * end - 1])
         + from_above
     )
+    leaf_sums(lambda rows: image[rows, :], bulk_store(last))
+    pair_late = remote(
+        bulk_send.at[1 - core, :, last], pair_recv.at[:, last], pair_s.at[1], pair_r.at[1], sibling
+    )
+    pair_late.start()
     for copy in copies1:
         copy.wait_send()
 
@@ -262,10 +285,11 @@
     ])
     recv3[w] = placed
 
-    leaf_sums(lambda rows: image[rows, :], bulk_store(last))
+    pair_late.wait_recv()
+    pair_add(last)
     copies10 = start_all([
-        remote(bulk_send.at[t, last], bulk_recv.at[d, last], s10.at[d], r10.at[d], (w, t))
-        for d, t in enumerate(subs)
+        remote(pair_sums.at[t, last], bulk_recv.at[d, last], s10.at[d], r10.at[d], (w, 2 * t + core))
+        for t, d in columns_z
     ])
 
     loads["eval"].wait()
@@ -325,8 +349,8 @@
     for copy in copies8 + copies10:
         copy.wait_recv()
     for j in range(BASIS):
-        total = bulk_send[s, j].astype(F32)
-        for d in range(SUB - 1):
+        total = pair_sums[s // 2, j].astype(F32)
+        for d in range(SUB // 2 - 1):
             total = total + bulk_recv[d, j].astype(F32)
         bulk_sums[j] = total
     area = area_send[s]
@@ -366,7 +390,7 @@
     ])
     for name in ("route_s", "slot_s"):
         loads[name].wait()
-    for copy in copies4 + copies8 + copies10:
+    for copy in copies4 + copies8 + copies10 + [pair_early, pair_late]:
         copy.wait_send()
 
     for d, v in enumerate(wide_sources):
@@ -457,8 +481,8 @@
     vector, hessenberg = pl.pallas_call(
         kernel,
         out_shape=(
-            jax.ShapeDtypeStruct((ROWS, NODES), F32),
-            jax.ShapeDtypeStruct((BASIS + 1, RHS), F32),
+            pltpu.VMEM((ROWS, NODES), F32),
+            pltpu.VMEM((BASIS + 1, RHS), F32),
         ),
         in_specs=[outside] * 10,
         out_specs=(inside, inside),
@@ -499,8 +523,10 @@
             pltpu.VMEM((SUB, RHS // 2, NODES), F32),
             pltpu.VMEM((RHS // 2, NODES), F32),
             pltpu.VMEM((WIDE, RHS // 2, NODES), F32),
-            pltpu.VMEM((SUB, BASIS, RHS * LEAVES, NODES), BF16),
-            pltpu.VMEM((SUB - 1, BASIS, RHS * LEAVES, NODES), BF16),
+            pltpu.VMEM((2, SUB // 2, BASIS, RHS * LEAVES, NODES), BF16),
+            pltpu.VMEM((SUB // 2, BASIS, RHS * LEAVES, NODES), BF16),
+            pltpu.VMEM((SUB // 2, BASIS, RHS * LEAVES, NODES), BF16),
+            pltpu.VMEM((SUB // 2 - 1, BASIS, RHS * LEAVES, NODES), BF16),
             pltpu.VMEM((BASIS, RHS * LEAVES, NODES), F32),
             pltpu.VMEM((SUB, LEAVES, NODES), F32),
             pltpu.VMEM((SUB - 1, LEAVES, NODES), F32),
@@ -512,9 +538,10 @@
             dma((SUB - 1,)), dma((SUB,)),
             dma((SUB - 1,)), dma((SUB,)),
             dma((WIDE - 1,)), dma((WIDE,)),
+            dma((SUB // 2 - 1,)), dma((SUB // 2 - 1,)),
             dma((SUB - 1,)), dma((SUB - 1,)),
-            dma((SUB - 1,)), dma((SUB - 1,)),
-            dma((SUB - 1,)), dma((SUB - 1,)),
+            dma((SUB // 2 - 1,)), dma((SUB // 2 - 1,)),
+            dma((2,)), dma((2,)),
         ],
         compiler_params=pltpu.CompilerParams(
             collective_id=0, has_side_effects=True, vmem_limit_bytes=60 << 20

time: 47.6 us -> 42.4 us (0.89)
  Pallas kernels: 43.3 us -> 40.1 us
  local copies, waits for them, and re-layouts: 3.53 us -> 1.56 us
    pallas_call x1, Pallas kernels: 43.3 us -> 40.1 us  [per_device(): pl.pallas_call(kernel, out_shape=(pltpu.VMEM((ROWS, NODES), F32), pltpu.V...]
    unnamed x2, local copies, waits for them, and re-layouts: 3.53 us -> 1.56 us
where the time goes in v3:
time: 42.4 us; the launch traced here: 42.3 us
  Pallas kernels  40.1 us (95%)
  local copies, waits for them, and re-layouts  1.56 us (4%)
  between operations  0.64 us (2%)
    pallas_call x1, Pallas kernels, per_device(): pl.pallas_call(kernel, out_shape=(pltpu.VMEM((ROWS, NODES), F32), pltpu.V...  40.1 us
    unnamed x2, local copies, waits for them, and re-layouts  1.56 us

profile of v3, /device:TPU:1, one launch (start us, length us, event | category | flops | bytes accessed | tf_op | source)
XLA Modules:
  0.0 42.3 jit_solution(14780247838786527734)
XLA Ops:
  0.6 40.1 %shard_map.113 = (f32[2048,128]{1,0:T(8,128)S(1)}, f32[5,16]{1,0:T(8,128)S(1)}) custom-call(f32[4,2048,128]{2,1,0:T(8,128)} %bitcast.8, f32[128,128]{1,0:T(8,128)} %weight_hbm.1, bf16[384,128,128]{2,1,0:T(8,128)(2,1)} %bitcast.7, s32[1,128]{1,0:T(1,128)} %bitcast.10, s32[1,128]{1,0:T(1,128)} %bitcast.11, bf16[128,256]{1,0:T(8,128)(2,1)} %multi_hbm.1, ...), custom_call_target="tpu_custom_call" | custom-call | tf_op jit(solution)/shard_map/pallas_call | solution.py:481
  40.7 1.0 %copy.14 = f32[128,16,128]{2,1,0:T(8,128)} copy(f32[128,16,128]{2,1,0:T(8,128)S(1)} %bitcast.6) | data formatting | bytes 2097152
  41.7 0.6 %copy.15 = f32[5,16]{1,0:T(8,128)} copy(f32[5,16]{1,0:T(8,128)S(1)} %get-tuple-element.7) | data formatting | bytes 640

commit v4 on v3

--- a/solution.py
+++ b/solution.py
@@ -16,6 +16,8 @@
 ROWS = PATCHES * RHS
 TOTAL = float(WIDE * SUB * PATCHES * NODES)
 SCALE = 1.0 / 32.0
+PACK = NODES // RHS
+DEVICES = WIDE * SUB
 PAIRS = [(j, k) for j in range(BASIS) for k in range(j, BASIS)]
 NEAR_CHUNKS = 4
 
@@ -46,8 +48,8 @@
     basis, weight, corr, route_v, slot_v, route_s, slot_s, multi, up, far, down, evalm, edge_corr,
     up_high, up_low, far_high, far_low, down_high, down_low, image,
     send1, recv1, sums1, send2, recv2, send3, recv3, send4, recv4, field,
-    edge_send, edge_recv, send6, recv6, send7, recv7, bulk_send, pair_recv, pair_sums, bulk_recv, bulk_sums, area_send, area_recv,
-    load_sem, corr_sem, edge_s, edge_r, s1, r1, s2, r2, s3, r3, s4, r4, s5, r5, s6, r6, s7, r7,
+    edge_send, edge_recv, send7, recv7, bulk_send, pair_recv, pair_sums, bulk_recv, bulk_sums, area_send, area_recv,
+    load_sem, corr_sem, edge_s, edge_r, s1, r1, s2, r2, s3, r3, s4, r4, s5, r5, s7, r7,
     s8, r8, s9, r9, s10, r10, pair_s, pair_r,
 ):
     w = lax.axis_index("wide")
@@ -315,9 +317,17 @@
         return tuple(a + weighted[j] * vectors[k] for a, (j, k) in zip(sums, PAIRS))
 
     gram = lax.fori_loop(0, PATCHES, gram_body, (zero,) * len(PAIRS), unroll=2)
-    packed = zero
-    for i, value in enumerate(gram):
-        packed = jnp.where(lane == BASIS + 1 + i, jnp.sum(value, axis=1, keepdims=True), packed)
+    row = lax.broadcasted_iota(jnp.int32, (RHS, NODES), 0)
+    spots = [(lane // RHS == m) & (lane % RHS == row) for m in range(PACK)]
+
+    def pack(tiles, first, values):
+        tiles = list(tiles)
+        for i, value in enumerate(values, first):
+            total = jnp.sum(value, axis=1, keepdims=True)
+            tiles[i // PACK] = jnp.where(spots[i % PACK], total, tiles[i // PACK])
+        return tiles
+
+    packed = pack([zero, zero], BASIS + 1, gram)
     for copy in copies2:
         copy.wait_send()
 
@@ -375,34 +385,32 @@
     products = [products[j] + far_sums[j] * (1.0 / SCALE) for j in range(BASIS)] + [
         products[BASIS] + far_sums[BASIS] * (2.0 / SCALE) + far_sums[BASIS + 1]
     ]
-    for i, value in enumerate(products):
-        packed = jnp.where(lane == i, jnp.sum(value, axis=1, keepdims=True), packed)
-    low_rows = RHS // 2
-    share = packed[:low_rows] + pltpu.roll(packed[low_rows:], RHS, 1)
-    send7[...] = share
-    copies7 = start_all([
-        remote(send7, recv7.at[w], s7.at[d], r7.at[w], (v, s)) for d, v in enumerate(wides)
-    ])
-    recv7[w] = share
+    packed = pack(packed, 0, products)
+    for a in range(2):
+        send7[a:a + 1, :] = jnp.sum(packed[a], axis=0, keepdims=True)
+
     own = pl.ds(s * LEAVES, LEAVES)
     copies5 = start_all([
         remote(field.at[own], field.at[own], s5.at[d], r5.at[s], (w, t)) for d, t in enumerate(subs)
     ])
+
+    def share(v, t):
+        return remote(send7, recv7.at[me], s7.at[0], r7.at[0], (v, t))
+
+    def share_wide(d, carry):
+        v = lax.rem(w + d, WIDE)
+        for e in range(SUB):
+            share(v, lax.rem(s + e, SUB)).start()
+        return carry
+
+    lax.fori_loop(1, WIDE, share_wide, 0)
+    for t in subs:
+        share(w, t).start()
+    recv7[me] = send7[...]
     for name in ("route_s", "slot_s"):
         loads[name].wait()
     for copy in copies4 + copies8 + copies10 + [pair_early, pair_late]:
         copy.wait_send()
-
-    for d, v in enumerate(wide_sources):
-        remote(send7, recv7.at[v], s7.at[d], r7.at[v], (v, s)).wait_recv()
-    total7 = recv7[0]
-    for v in range(1, WIDE):
-        total7 = total7 + recv7[v]
-    send6[...] = total7
-    copies6 = start_all([
-        remote(send6, recv6.at[s], s6.at[d], r6.at[s], (w, t)) for d, t in enumerate(subs)
-    ])
-    recv6[s] = total7
 
     for d in range(1, SUB):
         t = lax.rem(s + SUB - d, SUB)
@@ -416,19 +424,16 @@
         return carry
 
     lax.fori_loop(0, PATCHES, add_far, 0, unroll=4)
-    for copy in copies5 + copies7:
+    for copy in copies5:
         copy.wait_send()
-    for d in range(1, SUB):
-        t = lax.rem(s + SUB - d, SUB)
-        remote(send6, recv6.at[t], s6.at[d - 1], r6.at[t], (w, t)).wait_recv()
-    total7 = recv6[0]
-    for t in range(1, SUB):
-        total7 = total7 + recv6[t]
-    total7 = total7 * (1.0 / TOTAL)
-    full = jnp.concatenate([total7, pltpu.roll(total7, NODES - RHS, 1)], axis=0)
+    others = recv7.at[pl.ds(0, DEVICES - 1)]
+    everyone = remote(others, others, s7.at[0], r7.at[0], sibling)
+    everyone.wait_recv()
+    totals = jnp.sum(recv7[...], axis=0) * (1.0 / TOTAL)
+    wholes = [jnp.broadcast_to(totals[a:a + 1], (RHS, NODES)) for a in range(2)]
 
     def column(i):
-        return full[:, i:i + 1]
+        return jnp.sum(jnp.where(spots[i % PACK], wholes[i // PACK], 0.0), axis=1, keepdims=True)
 
     gram_of = {}
     for i, (j, k) in enumerate(PAIRS):
@@ -461,13 +466,11 @@
         return carry
 
     lax.fori_loop(0, PATCHES, final_body, 0, unroll=4)
-    row = lax.broadcasted_iota(jnp.int32, (RHS, NODES), 0)
     columns = coeffs + [beta]
     for i, value in enumerate(columns):
         flat = jnp.sum(jnp.where(row == lane, value, 0.0), axis=0, keepdims=True)
         hess_out[i:i + 1, :] = flat[:, :RHS]
-    for copy in copies6:
-        copy.wait_send()
+    everyone.wait_send()
 
 
 def per_device(
@@ -519,10 +522,8 @@
             pltpu.VMEM((SUB * LEAVES, RHS, NODES), BF16),
             pltpu.VMEM((2, RHS, NODES), F32),
             pltpu.VMEM((2, RHS, NODES), F32),
-            pltpu.VMEM((RHS // 2, NODES), F32),
-            pltpu.VMEM((SUB, RHS // 2, NODES), F32),
-            pltpu.VMEM((RHS // 2, NODES), F32),
-            pltpu.VMEM((WIDE, RHS // 2, NODES), F32),
+            pltpu.VMEM((2, NODES), F32),
+            pltpu.VMEM((DEVICES, 2, NODES), F32),
             pltpu.VMEM((2, SUB // 2, BASIS, RHS * LEAVES, NODES), BF16),
             pltpu.VMEM((SUB // 2, BASIS, RHS * LEAVES, NODES), BF16),
             pltpu.VMEM((SUB // 2, BASIS, RHS * LEAVES, NODES), BF16),
@@ -536,8 +537,7 @@
             dma((WIDE - 1,)), dma((WIDE,)),
             dma((SUB - 1,)), dma((SUB - 1,)),
             dma((SUB - 1,)), dma((SUB,)),
-            dma((SUB - 1,)), dma((SUB,)),
-            dma((WIDE - 1,)), dma((WIDE,)),
+            dma((1,)), dma((1,)),
             dma((SUB // 2 - 1,)), dma((SUB // 2 - 1,)),
             dma((SUB - 1,)), dma((SUB - 1,)),
             dma((SUB // 2 - 1,)), dma((SUB // 2 - 1,)),

time: 42.4 us -> 39.7 us (0.936)
  Pallas kernels: 40.1 us -> 37.4 us
    pallas_call x1, Pallas kernels: 40.1 us -> 37.4 us  [per_device(): pl.pallas_call(kernel, out_shape=(pltpu.VMEM((ROWS, NODES), F32), pltpu.V...]
where the time goes in v4:
time: 39.7 us; the launch traced here: 39.6 us
  Pallas kernels  37.4 us (94%)
  local copies, waits for them, and re-layouts  1.56 us (4%)
  between operations  0.64 us (2%)
    pallas_call x1, Pallas kernels, per_device(): pl.pallas_call(kernel, out_shape=(pltpu.VMEM((ROWS, NODES), F32), pltpu.V...  37.4 us
    unnamed x2, local copies, waits for them, and re-layouts  1.56 us

profile of v4, /device:TPU:1, one launch (start us, length us, event | category | flops | bytes accessed | tf_op | source)
XLA Modules:
  0.0 39.6 jit_solution(2429088701223642189)
XLA Ops:
  0.6 37.4 %shard_map.113 = (f32[2048,128]{1,0:T(8,128)S(1)}, f32[5,16]{1,0:T(8,128)S(1)}) custom-call(f32[4,2048,128]{2,1,0:T(8,128)} %bitcast.8, f32[128,128]{1,0:T(8,128)} %weight_hbm.1, bf16[384,128,128]{2,1,0:T(8,128)(2,1)} %bitcast.7, s32[1,128]{1,0:T(1,128)} %bitcast.10, s32[1,128]{1,0:T(1,128)} %bitcast.11, bf16[128,256]{1,0:T(8,128)(2,1)} %multi_hbm.1, ...), custom_call_target="tpu_custom_call" | custom-call | tf_op jit(solution)/shard_map/pallas_call | solution.py:484
  38.0 1.0 %copy.14 = f32[128,16,128]{2,1,0:T(8,128)} copy(f32[128,16,128]{2,1,0:T(8,128)S(1)} %bitcast.6) | data formatting | bytes 2097152
  39.0 0.6 %copy.15 = f32[5,16]{1,0:T(8,128)} copy(f32[5,16]{1,0:T(8,128)S(1)} %get-tuple-element.7) | data formatting | bytes 640

commit v5 on v4

--- a/solution.py
+++ b/solution.py
@@ -50,7 +50,7 @@
     send1, recv1, sums1, send2, recv2, send3, recv3, send4, recv4, field,
     edge_send, edge_recv, send7, recv7, bulk_send, pair_recv, pair_sums, bulk_recv, bulk_sums, area_send, area_recv,
     load_sem, corr_sem, edge_s, edge_r, s1, r1, s2, r2, s3, r3, s4, r4, s5, r5, s7, r7,
-    s8, r8, s9, r9, s10, r10, pair_s, pair_r,
+    s8, r8, s9, r9, s10, r10, pair_s, pair_r, entered,
 ):
     w = lax.axis_index("wide")
     s = lax.axis_index("sub")
@@ -67,7 +67,10 @@
     wide_sources = [lax.rem(w + WIDE - d, WIDE) for d in range(1, WIDE)]
 
     barrier = pltpu.get_barrier_semaphore()
-    peers = [(w, t) for t in subs] + [(v, s) for v in wides] + [below_id, above_id]
+    side = 4
+    x_line = [(lax.rem(w + side * d, WIDE), s) for d in range(1, side)]
+    y_line = [(w // side * side + lax.rem(w + d, side), s) for d in range(1, side)]
+    peers = [(w, t) for t in subs] + x_line + y_line + [below_id, above_id]
     for peer in peers:
         pl.semaphore_signal(barrier, inc=1, device_id=peer, device_id_type=MESH)
 
@@ -138,6 +141,8 @@
     leaf_sums(lambda rows: basis[last, rows, :], store1)
 
     pl.semaphore_wait(barrier, len(peers))
+    for peer in x_line:
+        pl.semaphore_signal(entered, inc=1, device_id=peer, device_id_type=MESH)
     copies1 = start_all([
         remote(send1.at[t], recv1.at[d], s1.at[d], r1.at[d], (w, t)) for d, t in enumerate(subs)
     ])
@@ -218,10 +223,15 @@
         [sums1[pl.ds(leaf, RHS, stride=LEAVES), :] for leaf in range(LEAVES)], axis=1
     )
     tree = split_dot(lanes, up_high, up_low)
-    send2[0] = tree[:, :NODES]
-    send2[1] = tree[:, NODES:]
+    low_rows = RHS // 2
+    lane_low = lax.broadcasted_iota(jnp.int32, (low_rows, NODES), 1)
+    for h in range(2):
+        top = tree[:low_rows, h * NODES:(h + 1) * NODES]
+        bottom = tree[low_rows:, h * NODES:(h + 1) * NODES]
+        send2[2 * h] = jnp.where(lane_low < NODES // 2, top, pltpu.roll(bottom, NODES // 2, 1))
+        send2[2 * h + 1] = jnp.where(lane_low < NODES // 2, pltpu.roll(top, NODES // 2, 1), bottom)
     copies2 = start_all([
-        remote(send2.at[t // 4], recv2.at[d], s2.at[d], r2.at[d], (w, t)) for d, t in enumerate(subs)
+        remote(send2.at[t // 2], recv2.at[d], s2.at[d], r2.at[d], (w, t)) for d, t in enumerate(subs)
     ])
 
     def pair_add(j):
@@ -272,16 +282,16 @@
 
     for copy in copies2:
         copy.wait_recv()
-    half_tree = send2[s // 4]
+    half_tree = send2[s // 2]
     for d in range(SUB - 1):
         half_tree = half_tree + recv2[d]
     lane = lax.broadcasted_iota(jnp.int32, (RHS, NODES), 1)
-    mine = jnp.where(lane // SHARE == lax.rem(s, 4), half_tree, 0.0)
-    turn = lax.rem(lax.rem(w, 4) + 4 - lax.rem(s, 4), 4)
-    placed = mine
-    for k in range(1, 4):
-        placed = jnp.where(turn == k, pltpu.roll(mine, k * SHARE, 1), placed)
+    mine = jnp.where(lax.rem(lane_low // SHARE, 2) == core, half_tree, 0.0)
+    turn = lax.rem(w, 2) - core
+    placed = jnp.where(turn == 1, pltpu.roll(mine, SHARE, 1), mine)
+    placed = jnp.where(turn == -1, pltpu.roll(mine, NODES - SHARE, 1), placed)
     send3[...] = placed
+    pl.semaphore_wait(entered, len(x_line))
     copies3 = start_all([
         remote(send3, recv3.at[w], s3.at[d], r3.at[w], (v, s)) for d, v in enumerate(wides)
     ])
@@ -333,13 +343,14 @@
 
     for d, v in enumerate(wide_sources):
         remote(send3, recv3.at[v], s3.at[d], r3.at[v], (v, s)).wait_recv()
-    lanes = jnp.concatenate(
-        [
-            (recv3[4 * g] + recv3[4 * g + 1]) + (recv3[4 * g + 2] + recv3[4 * g + 3])
-            for g in range(WIDE // 4)
-        ],
-        axis=1,
-    )
+    tiles = []
+    for g in range(WIDE // 4):
+        first = recv3[4 * g] + recv3[4 * g + 1]
+        second = recv3[4 * g + 2] + recv3[4 * g + 3]
+        top = jnp.where(lane_low < NODES // 2, first, pltpu.roll(second, NODES // 2, 1))
+        bottom = jnp.where(lane_low < NODES // 2, pltpu.roll(first, NODES // 2, 1), second)
+        tiles.append(jnp.concatenate([top, bottom], axis=0))
+    lanes = jnp.concatenate(tiles, axis=1)
     send4[...] = split_dot(lanes, far_high, far_low)
     copies4 = start_all([
         remote(send4, recv4.at[d], s4.at[d], r4.at[d], (w, t)) for d, t in enumerate(subs)
@@ -513,10 +524,10 @@
             pltpu.VMEM((SUB, RHS * LEAVES, NODES), BF16),
             pltpu.VMEM((SUB - 1, RHS * LEAVES, NODES), BF16),
             pltpu.VMEM((RHS * LEAVES, NODES), F32),
-            pltpu.VMEM((2, RHS, NODES), F32),
-            pltpu.VMEM((SUB - 1, RHS, NODES), F32),
-            pltpu.VMEM((RHS, NODES), F32),
-            pltpu.VMEM((WIDE, RHS, NODES), F32),
+            pltpu.VMEM((4, RHS // 2, NODES), F32),
+            pltpu.VMEM((SUB - 1, RHS // 2, NODES), F32),
+            pltpu.VMEM((RHS // 2, NODES), F32),
+            pltpu.VMEM((WIDE, RHS // 2, NODES), F32),
             pltpu.VMEM((RHS, COEFFS), F32),
             pltpu.VMEM((SUB - 1, RHS, COEFFS), F32),
             pltpu.VMEM((SUB * LEAVES, RHS, NODES), BF16),
@@ -542,6 +553,7 @@
             dma((SUB - 1,)), dma((SUB - 1,)),
             dma((SUB // 2 - 1,)), dma((SUB // 2 - 1,)),
             dma((2,)), dma((2,)),
+            pltpu.SemaphoreType.REGULAR,
         ],
         compiler_params=pltpu.CompilerParams(
             collective_id=0, has_side_effects=True, vmem_limit_bytes=60 << 20

time: 39.7 us -> 38.8 us (0.977)
  Pallas kernels: 37.4 us -> 36.5 us
    pallas_call x1, Pallas kernels: 37.4 us -> 36.5 us  [per_device(): pl.pallas_call(kernel, out_shape=(pltpu.VMEM((ROWS, NODES), F32), pltpu.V...]
where the time goes in v5:
time: 38.8 us; the launch traced here: 38.7 us
  Pallas kernels  36.5 us (94%)
  local copies, waits for them, and re-layouts  1.56 us (4%)
  between operations  0.64 us (2%)
    pallas_call x1, Pallas kernels, per_device(): pl.pallas_call(kernel, out_shape=(pltpu.VMEM((ROWS, NODES), F32), pltpu.V...  36.5 us
    unnamed x2, local copies, waits for them, and re-layouts  1.56 us

profile of v5, /device:TPU:1, one launch (start us, length us, event | category | flops | bytes accessed | tf_op | source)
XLA Modules:
  0.0 38.7 jit_solution(1969448922933873333)
XLA Ops:
  0.6 36.5 %shard_map.113 = (f32[2048,128]{1,0:T(8,128)S(1)}, f32[5,16]{1,0:T(8,128)S(1)}) custom-call(f32[4,2048,128]{2,1,0:T(8,128)} %bitcast.8, f32[128,128]{1,0:T(8,128)} %weight_hbm.1, bf16[384,128,128]{2,1,0:T(8,128)(2,1)} %bitcast.7, s32[1,128]{1,0:T(1,128)} %bitcast.10, s32[1,128]{1,0:T(1,128)} %bitcast.11, bf16[128,256]{1,0:T(8,128)(2,1)} %multi_hbm.1, ...), custom_call_target="tpu_custom_call" | custom-call | tf_op jit(solution)/shard_map/pallas_call | solution.py:495
  37.1 1.0 %copy.14 = f32[128,16,128]{2,1,0:T(8,128)} copy(f32[128,16,128]{2,1,0:T(8,128)S(1)} %bitcast.6) | data formatting | bytes 2097152
  38.1 0.6 %copy.15 = f32[5,16]{1,0:T(8,128)} copy(f32[5,16]{1,0:T(8,128)S(1)} %get-tuple-element.7) | data formatting | bytes 640

commit v6 on v5

--- a/solution.py
+++ b/solution.py
@@ -247,8 +247,6 @@
             pair_sums.at[t, early], bulk_recv.at[d, early], s8.at[d], r8.at[d], (w, 2 * t + core)
         )
         for t, d in columns_z
-    ] + [
-        remote(area_send.at[t], area_recv.at[d], s9.at[d], r9.at[d], (w, t)) for d, t in enumerate(subs)
     ])
 
     loads["far"].wait()
@@ -302,6 +300,8 @@
     copies10 = start_all([
         remote(pair_sums.at[t, last], bulk_recv.at[d, last], s10.at[d], r10.at[d], (w, 2 * t + core))
         for t, d in columns_z
+    ] + [
+        remote(area_send.at[t], area_recv.at[d], s9.at[d], r9.at[d], (w, t)) for d, t in enumerate(subs)
     ])
 
     loads["eval"].wait()

time: 38.8 us -> 38.8 us (level)
  no operation moved by 1% of the time
where the time goes in v6:
time: 38.8 us; the launch traced here: 38.7 us
  Pallas kernels  36.5 us (94%)
  local copies, waits for them, and re-layouts  1.56 us (4%)
  between operations  0.64 us (2%)
    pallas_call x1, Pallas kernels, per_device(): pl.pallas_call(kernel, out_shape=(pltpu.VMEM((ROWS, NODES), F32), pltpu.V...  36.5 us
    unnamed x2, local copies, waits for them, and re-layouts  1.56 us

profile of v6, /device:TPU:1, one launch (start us, length us, event | category | flops | bytes accessed | tf_op | source)
XLA Modules:
  0.0 38.7 jit_solution(2132880851844288405)
XLA Ops:
  0.6 36.5 %shard_map.113 = (f32[2048,128]{1,0:T(8,128)S(1)}, f32[5,16]{1,0:T(8,128)S(1)}) custom-call(f32[4,2048,128]{2,1,0:T(8,128)} %bitcast.8, f32[128,128]{1,0:T(8,128)} %weight_hbm.1, bf16[384,128,128]{2,1,0:T(8,128)(2,1)} %bitcast.7, s32[1,128]{1,0:T(1,128)} %bitcast.10, s32[1,128]{1,0:T(1,128)} %bitcast.11, bf16[128,256]{1,0:T(8,128)(2,1)} %multi_hbm.1, ...), custom_call_target="tpu_custom_call" | custom-call | tf_op jit(solution)/shard_map/pallas_call | solution.py:495
  37.1 1.0 %copy.14 = f32[128,16,128]{2,1,0:T(8,128)} copy(f32[128,16,128]{2,1,0:T(8,128)S(1)} %bitcast.6) | data formatting | bytes 2097152
  38.1 0.6 %copy.15 = f32[5,16]{1,0:T(8,128)} copy(f32[5,16]{1,0:T(8,128)S(1)} %get-tuple-element.7) | data formatting | bytes 640
